TPU v7x, 32 devices: a whole 2x2x4 slice. The times are simulated.
32 devices in a mesh: ctx: 8 (over z, y), head: 4 (over x, core).
Axes of the slice: x: 2, y: 2, z: 4, core: 2. Of those that a mesh axis runs over, the one named last changes fastest.
Arguments:
- queries: bfloat16 [1024, 73728], P('ctx', 'head'), may hold values from -6 to 6
- latent: bfloat16 [1024, 576], P('ctx'), may hold values from -6 to 6
- gate: float32 [1024, 128], P('ctx', 'head'), may hold values from -6 to 6
- d_out: bfloat16 [1024, 65536], P('ctx', 'head'), may hold values from -6 to 6
- segments: int32 [1024], replicated, may hold values from 0 to 15, never falling along the last dimension, each value on 1 to 128 neighbouring positions
Outputs:
- d_queries: bfloat16 [1024, 73728], P('ctx', 'head')
- d_gate: float32 [1024, 128], P('ctx', 'head')
- d_latent: float32 [1024, 576], P('ctx')
Inputs may be any that keep to these rules, and one draw needn't show every extreme that they name: `segments`: ids never fall along the tokens; every document has 1 to 128 tokens, so it covers at most two neighbouring ctx shards.
All inputs are finite; a program needn't handle non-finite values.
Results may differ from a plain program's by a relative error of at most 0.013.
Values may be sent and summed in bfloat16 or wider, within the bound.
No kernel may reach another device: no remote copies, remote signals or barrier semaphores. Data moves between devices by JAX's collectives and lax.ppermute only.
A program may use at most 64 MiB of HBM per device.

v0:
```python
import jax
import jax.numpy as jnp
from jax import lax
from jax.sharding import PartitionSpec as P

LATENT = 512
ROPE = 64


SCALE = 192.0 ** (-0.5)
CAP = 20.0


def shifted(value, axis, steps):
    count = lax.axis_size(axis)
    first, last = (max(0, -steps), min(count, count - steps))
    return lax.ppermute(value, axis, [(source, source + steps) for source in range(first, last)])


def build_allowed(segments, shard_index, tok_rows):
    first_row = shard_index * tok_rows
    query_seg = lax.dynamic_slice_in_dim(segments, first_row, tok_rows)
    prior_seg = lax.dynamic_slice_in_dim(segments, jnp.maximum(first_row - tok_rows, 0), tok_rows)
    key_seg = jnp.concatenate([prior_seg, query_seg])
    query_pos = first_row + jnp.arange(tok_rows, dtype=jnp.int32)
    key_pos = first_row - tok_rows + jnp.arange(2 * tok_rows, dtype=jnp.int32)
    same_doc = key_seg[None, :] == query_seg[:, None]
    return same_doc & (key_pos[None, :] <= query_pos[:, None]) & (key_pos[None, :] >= 0)


def local_grads(query_blk, all_keys, gate_blk, cotangent, allowed):
    f32 = jnp.float32
    values = all_keys[:, :LATENT]
    raw = jnp.einsum("qhd,kd->hqk", query_blk, all_keys, preferred_element_type=f32) * SCALE
    squashed = jnp.tanh(raw / CAP)
    weights = jnp.where(allowed[None], jnp.exp(CAP * squashed), 0.0)
    probs = weights / jnp.sum(weights, axis=2, keepdims=True)
    probs_low = probs.astype(jnp.bfloat16)
    attended = jnp.einsum("hqk,kd->qhd", probs_low, values, preferred_element_type=f32)
    opened = jax.nn.sigmoid(gate_blk)
    gate_grad = opened * (1.0 - opened) * jnp.sum(cotangent * attended, axis=2)
    d_att = (opened[:, :, None] * cotangent).astype(jnp.bfloat16)
    row_dot = jnp.sum(d_att * attended, axis=2)
    d_probs = jnp.einsum("qhd,kd->hqk", d_att, values, preferred_element_type=f32)
    d_raw = (
        probs * (d_probs - row_dot.T[:, :, None]) * (1.0 - squashed * squashed) * SCALE
    ).astype(jnp.bfloat16)
    d_query = jnp.einsum("hqk,kd->qhd", d_raw, all_keys, preferred_element_type=f32)
    d_keys = jnp.einsum("hqk,qhd->kd", d_raw, query_blk, preferred_element_type=f32)
    d_values = jnp.einsum("hqk,qhd->kd", probs_low, d_att, preferred_element_type=f32)
    d_total = d_keys + jnp.pad(d_values, ((0, 0), (0, ROPE)))
    return (d_query, gate_grad, d_total)


def shards(queries, latent, gate, d_out, segments):
    tok_rows = latent.shape[0]
    head_count = gate.shape[1]
    width = LATENT + ROPE
    shard_index = lax.axis_index("ctx")
    earlier_keys = shifted(latent, "ctx", 1)
    all_keys = jnp.concatenate([earlier_keys, latent], axis=0)
    allowed = build_allowed(segments, shard_index, tok_rows)
    d_query, gate_grad, d_total = local_grads(
        queries.reshape(tok_rows, head_count, width),
        all_keys,
        gate,
        d_out.reshape(tok_rows, head_count, LATENT),
        allowed,
    )
    earlier_part = d_total[:tok_rows]
    owned_part = d_total[tok_rows:]
    returned = shifted(earlier_part.astype(jnp.bfloat16), "ctx", -1).astype(earlier_part.dtype)
    column_share = lax.psum_scatter(owned_part + returned, "head", scatter_dimension=1, tiled=True)
    d_latent = lax.all_gather(column_share, "head", axis=1, tiled=True)
    d_queries = d_query.reshape(tok_rows, head_count * width).astype(jnp.bfloat16)
    return (d_queries, gate_grad, d_latent)


def solution(mesh):
    placed = (P("ctx", "head"), P("ctx", None), P("ctx", "head"), P("ctx", "head"), P())
    return jax.shard_map(
        shards,
        mesh=mesh,
        in_specs=placed,
        out_specs=(P("ctx", "head"), P("ctx", "head"), P("ctx", None)),
        check_vma=False,
    )
```

profile of v0, /device:TPU:0, one launch (start us, length us, event | category | flops | bytes accessed | tf_op | source)
XLA Modules:
  0.0 88.3 jit_solution(14449680965360314426)
XLA Ops:
  7.2 0.0 reduce-scatter.2.cloned.1.call-start
  7.2 4.9 %collective-permute-start = (bf16[128,576]{0,1:T(8,128)(2,1)}, bf16[128,576]{0,1:T(8,128)(2,1)S(1)}, u32[]{:S(2)}, u32[]{:S(2)}) collective-permute-start(bf16[128,576]{0,1:T(8,128)(2,1)} %param.6), channel_id=1, source_target_pairs={{0,4},{4,8},{8,12},{12,16},{16,20},{20,24},{24,28},{1,5},{5,9},{9,... | collective-permute-start | bytes 442376 | tf_op jit(solution)/shard_map/ppermute | solution.py:17
  12.1 6.6 %copy.19 = bf16[128,18432]{0,1:T(8,128)(2,1)} copy(bf16[128,18432]{1,0:T(8,128)(2,1)} %param.5) | data formatting | bytes 9437184 | tf_op args[0]
  18.7 7.1 %copy.20 = f32[128,16384]{0,1:T(8,128)} copy(bf16[128,16384]{1,0:T(8,128)(2,1)} %param.8) | data formatting | bytes 12582912 | tf_op jit(solution)/shard_map/convert_element_type | solution.py:42
  25.8 0.8 fusion.16
  26.7 0.2 and_and_fusion
  26.8 0.0 copy-done.1
  26.9 0.0 collective-permute-done
  26.9 0.0 copy-done
  26.9 0.0 slice-start
  27.0 0.0 slice-start.1
  27.0 5.1 %fusion.6 = (f32[32,128]{1,0:T(8,128)S(1)}, f32[256,128,32]{1,0,2:T(8,128)S(1)}) fusion(pred[128,256]{0,1:T(8,128)(4,1)S(1)} %and_and_fusion, bf16[128,32,576]{0,2,1:T(8,128)(2,1)} %bitcast.70, bf16[256,576]{0,1:T(8,128)(2,1)S(1)} %constant_dynamic-update-slice_fusion), kind=kOutput, calls=%fused_computation.13 | convolution fusion | flops 1212149760 | bytes 9256960 | tf_op jit(solution)/shard_map/qhd,kd->hqk/dot_general | solution.py:34
  32.1 0.0 slice-done
  32.2 0.0 slice-done.1
  32.2 4.6 %fusion.1 = (f32[128,32]{0,1:T(8,128)S(1)}, f32[128,32]{0,1:T(8,128)S(1)}, bf16[128,32,512]{0,2,1:T(8,128)(2,1)}) fusion(f32[128,16384]{0,1:T(8,128)S(1)} %bitcast.68, f32[128,32,512]{0,2,1:T(8,128)S(1)} %bitcast.69, f32[128,32]{0,1:T(8,128)S(1)} %add_divide_fusion, f32[256,128,32]{1,0,2:T(8,128)S(1)} %get-tuple-element.15, ...), kind=kOutput, calls=%fused_computation.3 | convolution fusion | flops 1093656576 | bytes 25526272 | tf_op jit(solution)/shard_map/hqk,kd->qhd/dot_general | solution.py:39
  36.8 3.9 %convolution_bitcast_fusion.1 = f32[256,512]{0,1:T(8,128)S(1)} fusion(bf16[128,32,512]{0,2,1:T(8,128)(2,1)} %get-tuple-element.11, f32[256,128,32]{1,0,2:T(8,128)S(1)} %get-tuple-element.15, f32[32,128]{1,0:T(8,128)S(1)} %get-tuple-element.14, pred[128,256]{0,1:T(8,128)(4,1)S(1)} %and_and_fusion), kind=kOutput, calls=%fused_computation.17 | convolution fusion | flops 1078984704 | bytes 8962048 | tf_op jit(solution)/shard_map/hqk,qhd->kd/dot_general | solution.py:50
  40.7 0.0 copy-done.2
  40.7 0.0 slice-start.3
  40.7 3.0 %fusion.3 = bf16[32,128,256]{1,2,0:T(8,128)(2,1)S(1)} fusion(f32[256,128,32]{1,0,2:T(8,128)S(1)} %get-tuple-element.15, bf16[128,32,512]{0,2,1:T(8,128)(2,1)S(1)} %copy-done.2, f32[32,128]{1,0:T(8,128)S(1)} %bitcast.74, f32[32,128]{1,0:T(8,128)S(1)} %get-tuple-element.14, pred[128,256]{0,1:T(8,128)(4,1)S(1)} %and_and_fusion, ...), kind=kOutput, calls=%fused_computation.7 | convolution fusion | flops 1085276160 | bytes 10813440 | tf_op jit(solution)/shard_map/qhd,kd->hqk/dot_general | solution.py:44
  43.7 0.0 slice-done.2
  43.7 0.0 slice-done.3
  43.7 1.4 %fusion.8 = f32[256,576]{0,1:T(8,128)S(1)} fusion(bf16[32,128,256]{1,2,0:T(8,128)(2,1)S(1)} %fusion.3, bf16[128,32,576]{0,2,1:T(8,128)(2,1)S(1)} %bitcast.73, f32[256,512]{0,1:T(8,128)S(1)} %convolution_bitcast_fusion.1), kind=kOutput, calls=%fused_computation.18 | convolution fusion | flops 1208107008 | bytes 7929856 | tf_op jit(solution)/shard_map/hqk,qhd->kd/dot_general | solution.py:49
  45.2 1.3 %collective-permute-start.1 = (bf16[128,576]{0,1:T(8,128)(2,1)S(1)}, bf16[128,576]{0,1:T(8,128)(2,1)S(1)}, u32[]{:S(2)}, u32[]{:S(2)}) collective-permute-start(bf16[128,576]{0,1:T(8,128)(2,1)S(1)} %slice.21), channel_id=1, source_target_pairs={{4,0},{8,4},{12,8},{16,12},{20,16},{24,20},{28,24},{5,1},{9,5},{13... | collective-permute-start | bytes 442376 | tf_op jit(solution)/shard_map/ppermute | solution.py:17
  46.5 5.9 %collective-permute-done.1 = bf16[128,576]{0,1:T(8,128)(2,1)S(1)} collective-permute-done((bf16[128,576]{0,1:T(8,128)(2,1)S(1)}, bf16[128,576]{0,1:T(8,128)(2,1)S(1)}, u32[]{:S(2)}, u32[]{:S(2)}) %collective-permute-start.1) | collective-permute-done | bytes 147488 | tf_op jit(solution)/shard_map/ppermute | solution.py:17
  52.4 0.7 slice_add_fusion
  53.1 0.0 reduce-scatter.2.cloned.1.call-update
  53.1 3.5 %convolution_convert_fusion = bf16[576,32,128]{2,0,1:T(8,128)(2,1)} fusion(bf16[32,128,256]{1,2,0:T(8,128)(2,1)S(1)} %fusion.3, bf16[256,576]{0,1:T(8,128)(2,1)S(1)} %constant_dynamic-update-slice_fusion), kind=kOutput, calls=%fused_computation.14 | convolution fusion | flops 1210318848 | bytes 7110656 | tf_op jit(solution)/shard_map/hqk,kd->qhd/dot_general | solution.py:48
  56.7 6.6 %copy.28 = bf16[128,18432]{1,0:T(8,128)(2,1)} copy(bf16[128,18432]{0,1:T(8,128)(2,1)} %bitcast.66) | data formatting | bytes 9437184
  63.3 0.6 fusion.13
  63.9 10.8 %reduce-scatter.2.cloned.1.call-done = f32[128,144]{0,1:T(8,128)} async-done(((f32[128,576]{0,1:T(8,128)}), f32[128,144]{0,1:T(8,128)}) %reduce-scatter.2.cloned.1.call-update) | async-done | bytes 73744 | tf_op jit(solution)/shard_map/reduce_scatter | solution.py:73
  74.7 6.1 %all_gather.3 = f32[128,576]{0,1:T(8,128)S(1)} all-gather(f32[128,144]{0,1:T(8,128)} %reduce-scatter.2.cloned.1.call-done), channel_id=1, replica_groups=mesh['ctx'=8,'head'=4] {'head'}, dimensions={1}, use_global_device_ids=true | all-gather | bytes 368640 | tf_op jit(solution)/shard_map/all_gather | solution.py:74
  80.8 0.7 copy.40
  (13 shorter events, 0.1 us)
Async XLA Ops:
  7.2 67.5 %reduce-scatter.2.cloned.1.call-start = ((), (), s32[]{:S(2)}) async-start(), calls=%async_computation.1 | async-start | bytes 368640 | tf_op jit(solution)/shard_map/reduce_scatter | solution.py:73
  7.2 19.7 %collective-permute-start = (bf16[128,576]{0,1:T(8,128)(2,1)}, bf16[128,576]{0,1:T(8,128)(2,1)S(1)}, u32[]{:S(2)}, u32[]{:S(2)}) collective-permute-start(bf16[128,576]{0,1:T(8,128)(2,1)} %param.6), channel_id=1, source_target_pairs={{0,4},{4,8},{8,12},{12,16},{16,20},{20,24},{24,28},{1,5},{5,9},{9,... | collective-permute-start | bytes 442376 | tf_op jit(solution)/shard_map/ppermute | solution.py:17
  18.7 8.1 %copy-start.1 = (f32[128,32]{0,1:T(8,128)S(1)}, f32[128,32]{0,1:T(8,128)}, u32[]{:S(2)}) copy-start(f32[128,32]{0,1:T(8,128)} %param.7) | copy-start | bytes 49156
  18.7 8.2 %copy-start = (bf16[128,576]{0,1:T(8,128)(2,1)S(1)}, bf16[128,576]{0,1:T(8,128)(2,1)}, u32[]{:S(2)}) copy-start(bf16[128,576]{0,1:T(8,128)(2,1)} %param.6) | copy-start | bytes 442372
  26.9 5.2 %slice-start = ((s8[8388608]{0:T(1024)(128)(4,1)}), s8[4194304]{0:T(1024)(128)(4,1)S(1)}, s32[]{:S(2)}) async-start(s8[8388608]{0:T(1024)(128)(4,1)} %bitcast.67), calls=%async_computation.2 | async-start | bytes 8388608
  27.0 5.2 %slice-start.1 = ((s8[8388608]{0:T(1024)(128)(4,1)}), s8[4194304]{0:T(1024)(128)(4,1)S(1)}, s32[]{:S(2)}) async-start(s8[8388608]{0:T(1024)(128)(4,1)} %bitcast.67), calls=%async_computation.3 | async-start | bytes 8388608
  36.8 3.9 %copy-start.2 = (bf16[128,32,512]{0,2,1:T(8,128)(2,1)S(1)}, bf16[128,32,512]{0,2,1:T(8,128)(2,1)}, u32[]{:S(2)}) copy-start(bf16[128,32,512]{0,2,1:T(8,128)(2,1)} %get-tuple-element.11) | copy-start | bytes 12582916
  36.8 6.9 %slice-start.2 = ((s8[4718592]{0:T(1024)(128)(4,1)}), s8[4194304]{0:T(1024)(128)(4,1)S(1)}, s32[]{:S(2)}) async-start(s8[4718592]{0:T(1024)(128)(4,1)} %bitcast.71), calls=%async_computation.4 | async-start | bytes 8388608
  40.7 3.0 %slice-start.3 = ((s8[4718592]{0:T(1024)(128)(4,1)}), s8[524288]{0:T(1024)(128)(4,1)S(1)}, s32[]{:S(2)}) async-start(s8[4718592]{0:T(1024)(128)(4,1)} %bitcast.71), calls=%async_computation.5 | async-start | bytes 1048576
  45.2 7.2 %collective-permute-start.1 = (bf16[128,576]{0,1:T(8,128)(2,1)S(1)}, bf16[128,576]{0,1:T(8,128)(2,1)S(1)}, u32[]{:S(2)}, u32[]{:S(2)}) collective-permute-start(bf16[128,576]{0,1:T(8,128)(2,1)S(1)} %slice.21), channel_id=1, source_target_pairs={{4,0},{8,4},{12,8},{16,12},{20,16},{24,20},{28,24},{5,1},{9,5},{13... | collective-permute-start | bytes 442376 | tf_op jit(solution)/shard_map/ppermute | solution.py:17
Sparse Core Ops, SparseCore 0:
  53.3 21.3 reduce-scatter.1
where the time goes:
time: 88.9 us; the launch traced here: 88.3 us
  local copies, waits for them, and re-layouts  22 us (25%)
  matrix products  21.6 us (24%)
  waiting for transfers between devices  16.7 us (19%)
  between operations  14.2 us (16%)
  starting transfers between devices  6.21 us (7%)
  blocking collectives  6.07 us (7%)
  other arithmetic  1.58 us (2%)
    unnamed x18, local copies, waits for them, and re-layouts  14 us
    reduce_scatter x1, waiting for transfers between devices, shards(): lax.psum_scatter(owned_part + returned, 'head', scatter_dimension=1, tile...  10.8 us
    convert_element_type x1, local copies, waits for them, and re-layouts, local_grads(): d_att = (opened[:, :, None] * cotangent).astype(jnp.bfloat16)  7.08 us
    ppermute x2, starting transfers between devices, shifted(): lax.ppermute(value, axis, [(source, source + steps) for source in range(f...  6.17 us
    all_gather x1, blocking collectives, shards(): d_latent = lax.all_gather(column_share, 'head', axis=1, tiled=True)  6.07 us
    ppermute x2, waiting for transfers between devices, shifted(): lax.ppermute(value, axis, [(source, source + steps) for source in range(f...  5.9 us
    dot_general x1, matrix products, local_grads(): jnp.einsum('qhd,kd->hqk', query_blk, all_keys, preferred_element_type=f32)  5.13 us
    dot_general x1, matrix products, local_grads(): jnp.einsum('hqk,kd->qhd', probs_low, values, preferred_element_type=f32)  4.59 us
  transfers between devices with their start and end apart: 3, of which 2 were waited for; matrix products, arithmetic and copies ran while one was open for 29% of the time, Pallas kernels for 0%

commit v1 on v0

v1 whole, which is shorter than its diff:
```python
import functools

import jax
import jax.numpy as jnp
from jax import lax
from jax.experimental import pallas as pl
from jax.experimental.pallas import tpu as pltpu
from jax.sharding import PartitionSpec as P

LATENT = 512
ROPE = 64
WIDTH = LATENT + ROPE
PAIR = 2 * WIDTH
PADDED = LATENT + 2 * ROPE
SCALE = 192.0 ** (-0.5)
CAP = 20.0
BF16 = jnp.bfloat16
F32 = jnp.float32


def dot_tt(a, b):
    return lax.dot_general(a, b, (((1,), (1,)), ((), ())), preferred_element_type=F32)


def dot_nn(a, b):
    return lax.dot_general(a, b, (((1,), (0,)), ((), ())), preferred_element_type=F32)


def padded_keys(keys_t):
    spare = jnp.zeros((ROPE, keys_t.shape[1]), keys_t.dtype)
    even = jnp.concatenate([keys_t, spare], axis=0).T
    odd = jnp.concatenate([spare, keys_t], axis=0).T
    return even, odd


def latent_grad_t(even, odd, values):
    first = even + jnp.concatenate([values, jnp.zeros((values.shape[0], 2 * ROPE), F32)], axis=1)
    return first.T[:WIDTH] + odd.T[ROPE:]


def head_slots(quad):
    return (4 * quad, 4 * quad + 2, 4 * quad + 1, 4 * quad + 3)


def own_scores(q_hbm, g_hbm, keys_t, scores, d_probs, q_all, g_all, sems):
    tok = keys_t.shape[1]
    quads = q_all.shape[0] // (2 * tok)
    copies = []
    for quad in range(quads):
        group = []
        for pair in (2 * quad, 2 * quad + 1):
            group.append((q_hbm.at[:, pl.ds(pair * PAIR, PAIR)], q_all.at[pl.ds(pair * tok, tok), :]))
        for slot, head in enumerate(head_slots(quad)):
            group.append(
                (g_hbm.at[:, pl.ds(head * LATENT, LATENT)], g_all.at[pl.ds((4 * quad + slot) * tok, tok), :])
            )
        copies.append([pltpu.make_async_copy(s, d, sems.at[quad, n]) for n, (s, d) in enumerate(group)])
        for copy in copies[-1]:
            copy.start()
    even, odd = padded_keys(keys_t[...])
    for quad in range(quads):
        for copy in copies[quad]:
            copy.wait()
        rows = pl.ds(quad * 2 * tok, 2 * tok)
        base = quad * 4 * tok
        scores[:, pl.ds(base, 2 * tok)] = dot_tt(even, q_all[rows, pl.ds(0, PADDED)])
        scores[:, pl.ds(base + 2 * tok, 2 * tok)] = dot_tt(odd, q_all[rows, pl.ds(LATENT, PADDED)])
        d_probs[:, pl.ds(base, 4 * tok)] = dot_tt(even[:, :LATENT], g_all[pl.ds(base, 4 * tok), :])


def prior_part(
    index, own_s, own_d, q_all, g_all, prior_t, gate_t, segments,
    d_raw, d_val, d_gate, early_t, acc_even, acc_odd, acc_val,
):
    tok = prior_t.shape[1]
    quads = q_all.shape[0] // (2 * tok)
    shard = index[0]
    even, odd = padded_keys(prior_t[...])
    row_own = segments[pl.ds(shard, 1), :]
    row_prior = segments[pl.ds(jnp.maximum(shard - 1, 0), 1), :]
    key_own = jnp.broadcast_to(row_own, (tok, tok)).T
    key_prior = jnp.broadcast_to(row_prior, (tok, tok)).T
    key_at = lax.broadcasted_iota(jnp.int32, (tok, tok), 0)
    query_at = lax.broadcasted_iota(jnp.int32, (tok, tok), 1)
    early = key_at > query_at
    same = jnp.where(early, key_prior, key_own) == row_own
    allowed = same & (jnp.logical_not(early) | (shard > 0))
    early = jnp.concatenate([early, early], axis=1)
    allowed = jnp.concatenate([allowed, allowed], axis=1)
    acc_even[...] = jnp.zeros_like(acc_even)
    acc_odd[...] = jnp.zeros_like(acc_odd)
    acc_val[...] = jnp.zeros_like(acc_val)

    def half(cols, heads, keys, q_blk, g_blk):
        raw = jnp.where(early, dot_tt(keys, q_blk), own_s[:, cols])
        d_p = jnp.where(early, dot_tt(even[:, :LATENT], g_blk), own_d[:, cols])
        squashed = jnp.tanh(raw * (SCALE / CAP))
        weights = jnp.where(allowed, jnp.exp(CAP * squashed), 0.0)
        total = jnp.sum(weights, axis=0, keepdims=True)
        opened = jax.nn.sigmoid(jnp.concatenate([gate_t[pl.ds(h, 1), :] for h in heads], axis=1))
        inverse = 1.0 / total
        mean = jnp.sum(weights * d_p, axis=0, keepdims=True) * inverse
        gate_grad = opened * (1.0 - opened) * mean
        for n, h in enumerate(heads):
            d_gate[pl.ds(h, 1), :] = gate_grad[:, n * tok : (n + 1) * tok]
        gated = weights * (inverse * opened)
        slope = gated * (d_p - mean) * (SCALE - SCALE * squashed * squashed)
        gated, slope = gated.astype(BF16), slope.astype(BF16)
        d_raw[:, cols] = slope
        d_val[:, cols] = gated
        zero = jnp.zeros_like(slope)
        return jnp.where(early, slope, zero), jnp.where(early, gated, zero)

    for quad in range(quads):
        rows = pl.ds(quad * 2 * tok, 2 * tok)
        base = quad * 4 * tok
        heads = head_slots(quad)
        for odd_half, keys, acc, at in ((0, even, acc_even, 0), (1, odd, acc_odd, LATENT)):
            cols = pl.ds(base + odd_half * 2 * tok, 2 * tok)
            q_blk = q_all[rows, pl.ds(at, PADDED)]
            g_blk = g_all[cols, :]
            slope, gated = half(cols, heads[2 * odd_half : 2 * odd_half + 2], keys, q_blk, g_blk)
            acc[...] += dot_nn(slope, q_blk)
            acc_val[...] += dot_nn(gated, g_blk)
    early_t[...] = latent_grad_t(acc_even[...], acc_odd[...], acc_val[...]).astype(early_t.dtype)


def own_part(d_raw, d_val, q_all, g_all, own_t, acc_even, acc_odd, acc_val):
    tok = d_raw.shape[0]
    quads = q_all.shape[0] // (2 * tok)
    key_at = lax.broadcasted_iota(jnp.int32, (tok, 2 * tok), 0)
    query_at = lax.broadcasted_iota(jnp.int32, (tok, 2 * tok), 1) % tok
    early = key_at > query_at
    acc_even[...] = jnp.zeros_like(acc_even)
    acc_odd[...] = jnp.zeros_like(acc_odd)
    acc_val[...] = jnp.zeros_like(acc_val)
    zero = jnp.zeros((tok, 2 * tok), BF16)
    for quad in range(quads):
        rows = pl.ds(quad * 2 * tok, 2 * tok)
        for odd_half, acc, at in ((0, acc_even, 0), (1, acc_odd, LATENT)):
            cols = pl.ds(quad * 4 * tok + odd_half * 2 * tok, 2 * tok)
            acc[...] += dot_nn(jnp.where(early, zero, d_raw[:, cols]), q_all[rows, pl.ds(at, PADDED)])
            acc_val[...] += dot_nn(jnp.where(early, zero, d_val[:, cols]), g_all[cols, :])
    own_t[...] = latent_grad_t(acc_even[...], acc_odd[...], acc_val[...])


def query_grads(d_raw, prior_t, keys_t, out_hbm, stage, sems):
    tok = d_raw.shape[0]
    quads = d_raw.shape[1] // (4 * tok)
    even_prior, odd_prior = padded_keys(prior_t[...])
    even_own, odd_own = padded_keys(keys_t[...])
    even = jnp.concatenate([even_prior, even_own], axis=0)
    odd = jnp.concatenate([odd_prior, odd_own], axis=0)
    middle = jnp.concatenate([even[:, LATENT:], odd[:, : 2 * ROPE]], axis=0)
    query_at = lax.broadcasted_iota(jnp.int32, (2 * tok, tok), 0) % tok
    key_at = lax.broadcasted_iota(jnp.int32, (2 * tok, tok), 1)
    early = key_at > query_at
    zero = jnp.zeros((2 * tok, tok), BF16)

    def unfolded(cols):
        slope = d_raw[:, cols].T
        return jnp.concatenate([jnp.where(early, slope, zero), jnp.where(early, zero, slope)], axis=1)

    def copies(quad):
        slot = quad % 2
        return [
            pltpu.make_async_copy(
                stage.at[slot, pl.ds(n * tok, tok), :],
                out_hbm.at[:, pl.ds((2 * quad + n) * PAIR, PAIR)],
                sems.at[slot, n],
            )
            for n in range(2)
        ]

    for quad in range(quads):
        if quad >= 2:
            for copy in copies(quad - 2):
                copy.wait()
        slot = quad % 2
        first = unfolded(pl.ds(quad * 4 * tok, 2 * tok))
        second = unfolded(pl.ds(quad * 4 * tok + 2 * tok, 2 * tok))
        stage[slot, :, pl.ds(0, LATENT)] = dot_nn(first, even[:, :LATENT]).astype(BF16)
        stage[slot, :, pl.ds(LATENT, 2 * ROPE)] = dot_nn(
            jnp.concatenate([first, second], axis=1), middle
        ).astype(BF16)
        stage[slot, :, pl.ds(LATENT + 2 * ROPE, LATENT)] = dot_nn(second, odd[:, 2 * ROPE :]).astype(BF16)
        for copy in copies(quad):
            copy.start()
    for quad in range(max(0, quads - 2), quads):
        for copy in copies(quad):
            copy.wait()


def shifted(value, axis, steps):
    count = lax.axis_size(axis)
    first, last = (max(0, -steps), min(count, count - steps))
    return lax.ppermute(value, axis, [(source, source + steps) for source in range(first, last)])


def shards(queries, latent, gate, d_out, segments):
    tok = latent.shape[0]
    heads = gate.shape[1]
    columns = heads * tok
    vmem = pl.BlockSpec(memory_space=pltpu.VMEM)
    smem = pl.BlockSpec(memory_space=pltpu.SMEM)
    hbm = pl.BlockSpec(memory_space=pl.ANY)
    params = pltpu.CompilerParams(vmem_limit_bytes=24 * 1024 * 1024)
    kept = pltpu.VMEM
    keys_t = latent.T
    gate_t = gate.T
    ids = segments.reshape(-1, tok)
    index = lax.axis_index("ctx").astype(jnp.int32).reshape(1)
    accumulators = [pltpu.VMEM((tok, PADDED), F32), pltpu.VMEM((tok, PADDED), F32), pltpu.VMEM((tok, LATENT), F32)]

    def cost(multiply_adds, moved):
        return pl.CostEstimate(flops=2 * multiply_adds, bytes_accessed=moved, transcendentals=0)

    prior_t = shifted(keys_t, "ctx", 1)
    own_s, own_d, q_all, g_all = pl.pallas_call(
        own_scores,
        out_shape=[
            kept((tok, columns), F32),
            kept((tok, columns), F32),
            kept((columns // 2, PAIR), BF16),
            kept((columns, LATENT), BF16),
        ],
        in_specs=[hbm, hbm, vmem],
        out_specs=[vmem] * 4,
        scratch_shapes=[pltpu.SemaphoreType.DMA((heads // 4, 6))],
        compiler_params=params,
        cost_estimate=cost(columns * tok * (PADDED + LATENT), queries.size * 2 + d_out.size * 2),
        name="own_scores",
    )(queries, d_out, keys_t)
    d_raw, d_val, d_gate_t, early_t = pl.pallas_call(
        prior_part,
        out_shape=[
            kept((tok, columns), BF16),
            kept((tok, columns), BF16),
            jax.ShapeDtypeStruct((heads, tok), F32),
            kept((WIDTH, tok), BF16),
        ],
        in_specs=[smem] + [vmem] * 7,
        out_specs=[vmem] * 4,
        scratch_shapes=accumulators,
        compiler_params=params,
        cost_estimate=cost(2 * columns * tok * (PADDED + LATENT), 0),
        name="prior_part",
    )(index, own_s, own_d, q_all, g_all, prior_t, gate_t, ids)
    returned = shifted(early_t, "ctx", -1)
    own_t = pl.pallas_call(
        own_part,
        out_shape=kept((WIDTH, tok), F32),
        in_specs=[vmem] * 4,
        out_specs=vmem,
        scratch_shapes=accumulators,
        compiler_params=params,
        cost_estimate=cost(columns * tok * (PADDED + LATENT), 0),
        name="own_part",
    )(d_raw, d_val, q_all, g_all)
    d_queries = pl.pallas_call(
        query_grads,
        out_shape=jax.ShapeDtypeStruct(queries.shape, queries.dtype),
        in_specs=[vmem] * 3,
        out_specs=hbm,
        scratch_shapes=[pltpu.VMEM((2, 2 * tok, PAIR), BF16), pltpu.SemaphoreType.DMA((2, 2))],
        compiler_params=params,
        cost_estimate=cost(columns * 2 * tok * PADDED, queries.size * 2),
        name="query_grads",
    )(d_raw, prior_t, keys_t)
    total = own_t + returned.astype(F32)
    group = lax.axis_size("head")
    step = 1
    while step < group:
        sent = total.astype(BF16)
        other = lax.ppermute(sent, "head", [(i, i ^ step) for i in range(group)])
        total = sent.astype(F32) + other.astype(F32)
        step *= 2
    return d_queries, d_gate_t.T, total.T


def solution(mesh):
    placed = (P("ctx", "head"), P("ctx", None), P("ctx", "head"), P("ctx", "head"), P())
    return jax.shard_map(
        shards,
        mesh=mesh,
        in_specs=placed,
        out_specs=(P("ctx", "head"), P("ctx", "head"), P("ctx", None)),
        check_vma=False,
    )
```

time: 88.9 us -> 40.9 us (0.46)
  matrix products: 21.6 us -> 0 us
  Pallas kernels: 0 us -> 20.3 us
  local copies, waits for them, and re-layouts: 22 us -> 5.43 us
  between operations: 14.2 us -> 0.74 us
  waiting for transfers between devices: 16.7 us -> 5.54 us
  blocking collectives: 6.07 us -> 0 us
  starting transfers between devices: 6.21 us -> 7.78 us
    dot_general x6 -> x0, matrix products: 21.6 us -> none  [the longest x1 5.13 us: local_grads(): jnp.einsum('qhd,kd->hqk', query_blk, all_keys, preferred_element_type=f32)]
    pallas_call x0 -> x4, Pallas kernels: none -> 20.3 us  [the longest x1 7.56 us: shards(): pl.pallas_call(prior_part, out_shape=[kept((tok, columns), BF16), kept((t...]
    reduce_scatter x1 -> x0, waiting for transfers between devices: 10.8 us -> none  [shards(): lax.psum_scatter(owned_part + returned, 'head', scatter_dimension=1, tile...]
    unnamed x18 -> x10, local copies, waits for them, and re-layouts: 14 us -> 5.43 us
    convert_element_type x1 -> x0, local copies, waits for them, and re-layouts: 7.08 us -> none  [local_grads(): d_att = (opened[:, :, None] * cotangent).astype(jnp.bfloat16)]
    all_gather x1 -> x0, blocking collectives: 6.07 us -> none  [shards(): d_latent = lax.all_gather(column_share, 'head', axis=1, tiled=True)]
    ppermute x2, waiting for transfers between devices: 5.9 us -> 4.18 us  [shifted(): lax.ppermute(value, axis, [(source, source + steps) for source in range(f...]
    ppermute x0 -> x2, starting transfers between devices: none -> 1.63 us  [shards(): other = lax.ppermute(sent, 'head', [(i, i ^ step) for i in range(group)])]
  transfers between devices with their start and end apart: 3 -> 4, of which waited for: 2 -> 2; matrix products, arithmetic and copies ran while one was open for 29% -> 0% of each run, Pallas kernels for 0% -> 31%
where the time goes in v1:
time: 40.9 us; the launch traced here: 40.7 us
  Pallas kernels  20.3 us (50%)
  starting transfers between devices  7.78 us (19%)
  waiting for transfers between devices  5.54 us (14%)
  local copies, waits for them, and re-layouts  5.43 us (13%)
  other arithmetic  0.83 us (2%)
  between operations  0.74 us (2%)
    pallas_call x1, Pallas kernels, shards(): pl.pallas_call(prior_part, out_shape=[kept((tok, columns), BF16), kept((t...  7.56 us
    ppermute x2, starting transfers between devices, shifted(): lax.ppermute(value, axis, [(source, source + steps) for source in range(f...  6.16 us
    pallas_call x1, Pallas kernels, shards(): pl.pallas_call(own_scores, out_shape=[kept((tok, columns), F32), kept((to...  5.76 us
    unnamed x10, local copies, waits for them, and re-layouts  5.43 us
    pallas_call x1, Pallas kernels, shards(): pl.pallas_call(query_grads, out_shape=jax.ShapeDtypeStruct(queries.shape,...  5.33 us
    ppermute x2, waiting for transfers between devices, shifted(): lax.ppermute(value, axis, [(source, source + steps) for source in range(f...  4.18 us
    pallas_call x1, Pallas kernels, shards(): pl.pallas_call(own_part, out_shape=kept((WIDTH, tok), F32), in_specs=[vme...  1.7 us
    ppermute x2, starting transfers between devices, shards(): other = lax.ppermute(sent, 'head', [(i, i ^ step) for i in range(group)])  1.63 us
  transfers between devices with their start and end apart: 4, of which 2 were waited for; matrix products, arithmetic and copies ran while one was open for 0% of the time, Pallas kernels for 31%

profile of v1, /device:TPU:0, one launch (start us, length us, event | category | flops | bytes accessed | tf_op | source)
XLA Modules:
  0.0 40.7 jit_solution(5264080405144536187)
XLA Ops:
  0.6 4.9 %collective-permute-start = (bf16[576,128]{1,0:T(8,128)(2,1)}, bf16[576,128]{1,0:T(8,128)(2,1)S(1)}, u32[]{:S(2)}, u32[]{:S(2)}) collective-permute-start(bf16[576,128]{1,0:T(8,128)(2,1)} %bitcast.7), channel_id=1, source_target_pairs={{0,4},{4,8},{8,12},{12,16},{16,20},{20,24},{24,28},{1,5},{5,9},{9,... | collective-permute-start | bytes 442376 | tf_op jit(solution)/shard_map/ppermute | solution.py:197
  5.5 0.0 copy-start
  5.5 2.3 %copy-done = bf16[128,18432]{1,0:T(8,128)(2,1)S(1)} copy-done((bf16[128,18432]{1,0:T(8,128)(2,1)S(1)}, bf16[128,18432]{1,0:T(8,128)(2,1)}, u32[]{:S(2)}) %copy-start) | copy-done | bytes 4718616
  7.9 0.0 copy-start.1
  7.9 2.2 %copy-done.1 = bf16[128,16384]{1,0:T(8,128)(2,1)S(1)} copy-done((bf16[128,16384]{1,0:T(8,128)(2,1)S(1)}, bf16[128,16384]{1,0:T(8,128)(2,1)}, u32[]{:S(2)}) %copy-start.1) | copy-done | bytes 4194328
  10.0 0.0 copy-start.2
  10.1 0.9 %copy-done.2 = bf16[128,576]{0,1:T(8,128)(2,1)S(1)} copy-done((bf16[128,576]{0,1:T(8,128)(2,1)S(1)}, bf16[128,576]{0,1:T(8,128)(2,1)}, u32[]{:S(2)}) %copy-start.2) | copy-done | bytes 147480
  11.0 0.0 copy-start.3
  11.0 0.0 copy-start.4
  11.0 5.8 %own_scores.1 = (f32[128,4096]{1,0:T(8,128)S(1)}, f32[128,4096]{1,0:T(8,128)S(1)}, bf16[2048,1152]{1,0:T(8,128)(2,1)S(1)}, bf16[4096,512]{1,0:T(8,128)(2,1)S(1)}) custom-call(bf16[128,18432]{1,0:T(8,128)(2,1)S(1)} %copy-done, bf16[128,16384]{1,0:T(8,128)(2,1)S(1)} %copy-done.1, bf16[576,128]{1,0:T(8,128)(2,1)S(1)} %bitcast.8), custom_call_target="tpu_custom_call" | custom-call | flops 1207959552 | bytes 8912896 | tf_op jit(solution)/shard_map/own_scores/pallas_call | solution.py:219
  16.7 0.0 collective-permute-done.prior_t
  16.7 0.0 copy-done.3
  16.8 0.0 copy-done.4
  16.8 7.6 %prior_part.1 = (bf16[128,4096]{1,0:T(8,128)(2,1)S(1)}, bf16[128,4096]{1,0:T(8,128)(2,1)S(1)}, f32[32,128]{1,0:T(8,128)}, bf16[576,128]{1,0:T(8,128)(2,1)S(1)}) custom-call(s32[1]{0:T(128)} %bitcast.index, f32[128,4096]{1,0:T(8,128)S(1)} %get-tuple-element.11.own_s, f32[128,4096]{1,0:T(8,128)S(1)} %get-tuple-element.12.own_d, ...), custom_call_target="tpu_custom_call" | custom-call | flops 2415919104 | tf_op jit(solution)/shard_map/prior_part/pallas_call | solution.py:234
  24.3 1.3 %collective-permute-start.1 = (bf16[576,128]{1,0:T(8,128)(2,1)S(1)}, bf16[576,128]{1,0:T(8,128)(2,1)S(1)}, u32[]{:S(2)}, u32[]{:S(2)}) collective-permute-start(bf16[576,128]{1,0:T(8,128)(2,1)S(1)} %get-tuple-element.18), channel_id=1, source_target_pairs={{4,0},{8,4},{12,8},{16,12},{20,16},{24,20},{28,24},{5,1},{9,5},{13... | collective-permute-start | bytes 442376 | tf_op jit(solution)/shard_map/ppermute | solution.py:197
  25.6 1.7 %own_part.1 = f32[576,128]{1,0:T(8,128)S(1)} custom-call(bf16[128,4096]{1,0:T(8,128)(2,1)S(1)} %get-tuple-element.15.d_raw, bf16[128,4096]{1,0:T(8,128)(2,1)S(1)} %get-tuple-element.17.d_val, bf16[2048,1152]{1,0:T(8,128)(2,1)S(1)} %get-tuple-element.13.q_all, bf16[4096,512]{1,0:T(8,128)(2,1)S(1)} %get-tuple-element.14.g_all), custom_call_target="tpu_custom_call" | custom-call | flops 1207959552 | tf_op jit(solution)/shard_map/own_part/pallas_call | solution.py:250
  27.3 4.2 %collective-permute-done.1 = bf16[576,128]{1,0:T(8,128)(2,1)S(1)} collective-permute-done((bf16[576,128]{1,0:T(8,128)(2,1)S(1)}, bf16[576,128]{1,0:T(8,128)(2,1)S(1)}, u32[]{:S(2)}, u32[]{:S(2)}) %collective-permute-start.1) | collective-permute-done | bytes 147488 | tf_op jit(solution)/shard_map/ppermute | solution.py:197
  31.5 0.1 collective-permute-start.2
  31.6 1.4 %collective-permute-done.2 = bf16[576,128]{1,0:T(8,128)(2,1)S(1)} collective-permute-done((bf16[576,128]{1,0:T(8,128)(2,1)S(1)}, bf16[576,128]{1,0:T(8,128)(2,1)S(1)}, u32[]{:S(2)}, u32[]{:S(2)}) %collective-permute-start.2) | collective-permute-done | bytes 147488 | tf_op jit(solution)/shard_map/ppermute | solution.py:275
  33.0 1.6 %collective-permute-start.3 = (bf16[576,128]{1,0:T(8,128)(2,1)S(1)}, bf16[576,128]{1,0:T(8,128)(2,1)S(1)}, u32[]{:S(2)}, u32[]{:S(2)}) collective-permute-start(bf16[576,128]{1,0:T(8,128)(2,1)S(1)} %add_convert_fusion), channel_id=1, source_target_pairs={{0,2},{1,3},{2,0},{3,1},{4,6},{5,7},{6,4},{7,5},{8,10},{9,11},{10,... | collective-permute-start | bytes 442376 | tf_op jit(solution)/shard_map/ppermute | solution.py:275
  34.6 5.3 %query_grads.1 = bf16[128,18432]{1,0:T(8,128)(2,1)} custom-call(bf16[128,4096]{1,0:T(8,128)(2,1)S(1)} %get-tuple-element.15.d_raw, bf16[576,128]{1,0:T(8,128)(2,1)S(1)} %collective-permute-done.prior_t, bf16[576,128]{1,0:T(8,128)(2,1)S(1)} %bitcast.9), custom_call_target="tpu_custom_call" | custom-call | flops 1342177280 | bytes 4718592 | tf_op jit(solution)/shard_map/query_grads/pallas_call | solution.py:260
  39.9 0.0 collective-permute-done.3
  39.9 0.7 %add_bitcast_fusion = f32[128,576]{0,1:T(8,128)} fusion(bf16[576,128]{1,0:T(8,128)(2,1)S(1)} %collective-permute-done.3, bf16[576,128]{1,0:T(8,128)(2,1)S(1)} %add_convert_fusion), kind=kLoop, calls=%fused_computation | loop fusion | flops 221184 | bytes 589824 | tf_op jit(solution)/shard_map/transpose | solution.py:278
  (2 shorter events, 0.1 us)
Async XLA Ops:
  0.6 16.1 %collective-permute-start = (bf16[576,128]{1,0:T(8,128)(2,1)}, bf16[576,128]{1,0:T(8,128)(2,1)S(1)}, u32[]{:S(2)}, u32[]{:S(2)}) collective-permute-start(bf16[576,128]{1,0:T(8,128)(2,1)} %bitcast.7), channel_id=1, source_target_pairs={{0,4},{4,8},{8,12},{12,16},{16,20},{20,24},{24,28},{1,5},{5,9},{9,... | collective-permute-start | bytes 442376 | tf_op jit(solution)/shard_map/ppermute | solution.py:197
  5.5 2.3 %copy-start = (bf16[128,18432]{1,0:T(8,128)(2,1)S(1)}, bf16[128,18432]{1,0:T(8,128)(2,1)}, u32[]{:S(2)}) copy-start(bf16[128,18432]{1,0:T(8,128)(2,1)} %q_hbm.1) | copy-start | bytes 14155780
  7.9 2.2 %copy-start.1 = (bf16[128,16384]{1,0:T(8,128)(2,1)S(1)}, bf16[128,16384]{1,0:T(8,128)(2,1)}, u32[]{:S(2)}) copy-start(bf16[128,16384]{1,0:T(8,128)(2,1)} %g_hbm.1) | copy-start | bytes 12582916
  10.0 0.9 %copy-start.2 = (bf16[128,576]{0,1:T(8,128)(2,1)S(1)}, bf16[128,576]{0,1:T(8,128)(2,1)}, u32[]{:S(2)}) copy-start(bf16[128,576]{0,1:T(8,128)(2,1)} %param.6) | copy-start | bytes 442372
  11.0 5.8 %copy-start.3 = (f32[128,32]{0,1:T(8,128)S(1)}, f32[128,32]{0,1:T(8,128)}, u32[]{:S(2)}) copy-start(f32[128,32]{0,1:T(8,128)} %param.7) | copy-start | bytes 49156
  11.0 5.8 %copy-start.4 = (s32[1024]{0:T(1024)S(1)}, s32[1024]{0:T(1024)}, u32[]{:S(2)}) copy-start(s32[1024]{0:T(1024)} %param.9) | copy-start | bytes 12292
  24.3 7.2 %collective-permute-start.1 = (bf16[576,128]{1,0:T(8,128)(2,1)S(1)}, bf16[576,128]{1,0:T(8,128)(2,1)S(1)}, u32[]{:S(2)}, u32[]{:S(2)}) collective-permute-start(bf16[576,128]{1,0:T(8,128)(2,1)S(1)} %get-tuple-element.18), channel_id=1, source_target_pairs={{4,0},{8,4},{12,8},{16,12},{20,16},{24,20},{28,24},{5,1},{9,5},{13... | collective-permute-start | bytes 442376 | tf_op jit(solution)/shard_map/ppermute | solution.py:197
  31.5 1.4 %collective-permute-start.2 = (bf16[576,128]{1,0:T(8,128)(2,1)S(1)}, bf16[576,128]{1,0:T(8,128)(2,1)S(1)}, u32[]{:S(2)}, u32[]{:S(2)}) collective-permute-start(bf16[576,128]{1,0:T(8,128)(2,1)S(1)} %add_convert_fusion.1), channel_id=1, source_target_pairs={{0,1},{1,0},{2,3},{3,2},{4,5},{5,4},{6,7},{7,6},{8,9},{9,8},{10,11... | collective-permute-start | bytes 442376 | tf_op jit(solution)/shard_map/ppermute | solution.py:275
  33.0 6.9 %collective-permute-start.3 = (bf16[576,128]{1,0:T(8,128)(2,1)S(1)}, bf16[576,128]{1,0:T(8,128)(2,1)S(1)}, u32[]{:S(2)}, u32[]{:S(2)}) collective-permute-start(bf16[576,128]{1,0:T(8,128)(2,1)S(1)} %add_convert_fusion), channel_id=1, source_target_pairs={{0,2},{1,3},{2,0},{3,1},{4,6},{5,7},{6,4},{7,5},{8,10},{9,11},{10,... | collective-permute-start | bytes 442376 | tf_op jit(solution)/shard_map/ppermute | solution.py:275

commit v2 on v0

v2 whole, which is shorter than its diff:
```python
import functools

import jax
import jax.numpy as jnp
from jax import lax
from jax.experimental import pallas as pl
from jax.experimental.pallas import tpu as pltpu
from jax.sharding import PartitionSpec as P

LATENT = 512
ROPE = 64
WIDTH = LATENT + ROPE
PAIR = 2 * WIDTH
PADDED = LATENT + 2 * ROPE
SCALE = 192.0 ** (-0.5)
CAP = 20.0
LATE = 3
LOG2_E = 1.4426950408889634
BF16 = jnp.bfloat16
F32 = jnp.float32


def dot_nn(a, b):
    return lax.dot_general(a, b, (((1,), (0,)), ((), ())), preferred_element_type=F32)


def padded_keys(keys_t):
    spare = jnp.zeros((ROPE, keys_t.shape[1]), keys_t.dtype)
    even = jnp.concatenate([keys_t, spare], axis=0).T
    odd = jnp.concatenate([spare, keys_t], axis=0).T
    return even, odd


AHEAD = 3


def head_slots(quad):
    return (4 * quad, 4 * quad + 2, 4 * quad + 1, 4 * quad + 3)


def turn(q_rows, g_rows, q_turned, g_turned, start, tok):
    for n in range(2):
        turned = q_rows[n * tok : (n + 1) * tok].T
        q_turned[:, pl.ds(start + n * tok, tok)] = turned[:WIDTH]
        q_turned[:, pl.ds(start + (2 + n) * tok, tok)] = turned[WIDTH:]
    for n in range(4):
        g_turned[:, pl.ds(start + n * tok, tok)] = g_rows[n * tok : (n + 1) * tok].T


def own_scores(
    q_hbm, g_hbm, keys_hbm,
    scores, d_probs, q_turned, g_turned, q_late, g_late, keys_t,
    q_early, g_early, sems, key_sem,
):
    tok = keys_t.shape[1]
    early, late = q_early.shape[0] // (2 * tok), q_late.shape[0] // (2 * tok)
    quads = early + late
    keys_copy = pltpu.make_async_copy(keys_hbm, keys_t, key_sem.at[0])
    keys_copy.start()

    def copies(quad):
        q_to, g_to, at = (q_early, g_early, quad) if quad < early else (q_late, g_late, quad - early)
        group = []
        for n in range(2):
            group.append(
                (q_hbm.at[:, pl.ds((2 * quad + n) * PAIR, PAIR)], q_to.at[pl.ds((2 * at + n) * tok, tok), :])
            )
        for slot, head in enumerate(head_slots(quad)):
            group.append((g_hbm.at[:, pl.ds(head * LATENT, LATENT)], g_to.at[pl.ds((4 * at + slot) * tok, tok), :]))
        return [pltpu.make_async_copy(s, d, sems.at[quad, n]) for n, (s, d) in enumerate(group)]

    def score(quad):
        for n in range(2):
            cols = pl.ds((4 * quad + 2 * n) * tok, 2 * tok)
            scores[:, cols] = dot_nn(keys, q_turned[:, cols])
            d_probs[:, cols] = dot_nn(keys[:, :LATENT], g_turned[:, cols])

    for quad in range(min(AHEAD, quads)):
        for copy in copies(quad):
            copy.start()
    keys_copy.wait()
    keys = keys_t[...].T
    for quad in range(early):
        if quad + AHEAD < quads:
            for copy in copies(quad + AHEAD):
                copy.start()
        for copy in copies(quad):
            copy.wait()
        turn(
            q_early[pl.ds(2 * quad * tok, 2 * tok), :], g_early[pl.ds(4 * quad * tok, 4 * tok), :],
            q_turned, g_turned, 4 * quad * tok, tok,
        )
        if quad > 0:
            score(quad - 1)
    for quad in range(early + AHEAD, quads):
        for copy in copies(quad):
            copy.start()
    score(early - 1)
    for quad in range(early, quads):
        for copy in copies(quad):
            copy.wait()


def grads(
    own_s, own_d, q_turned, g_turned, q_late, g_late, prior_t, keys_t, gate_t, segments,
    d_raw, d_gate, early_keep, own_keep, send, q_turned_late, g_turned_late, d_val, total,
):
    tok = prior_t.shape[1]
    early_quads, late_quads = q_turned.shape[1] // (4 * tok), q_late.shape[0] // (2 * tok)
    shard = lax.axis_index("ctx")
    prior_keys = prior_t[...].T
    all_keys = jnp.concatenate([prior_keys, keys_t[...].T], axis=0)
    row_own = segments[pl.ds(shard, 1), :]
    row_prior = segments[pl.ds(jnp.maximum(shard - 1, 0), 1), :]
    key_own = jnp.broadcast_to(row_own, (tok, tok)).T
    key_prior = jnp.broadcast_to(row_prior, (tok, tok)).T
    key_at = lax.broadcasted_iota(jnp.int32, (tok, tok), 0)
    query_at = lax.broadcasted_iota(jnp.int32, (tok, tok), 1)
    early = key_at > query_at
    same = jnp.where(early, key_prior, key_own) == row_own
    allowed = same & (jnp.logical_not(early) | (shard > 0))
    early = jnp.concatenate([early, early], axis=1)
    allowed = jnp.concatenate([allowed, allowed], axis=1)
    query_row = lax.broadcasted_iota(jnp.int32, (2 * tok, tok), 0) % tok
    key_column = lax.broadcasted_iota(jnp.int32, (2 * tok, tok), 1)
    early_row = key_column > query_row
    nothing = jnp.zeros((2 * tok, tok), BF16)
    total[...] = jnp.zeros_like(total)

    def place(n):
        quad, odd = n // 2, n % 2
        if quad < early_quads:
            return q_turned, g_turned, pl.ds(n * 2 * tok, 2 * tok)
        return q_turned_late, g_turned_late, pl.ds((n - 2 * early_quads) * 2 * tok, 2 * tok)

    def scores_of(n):
        q_from, g_from, cols = place(n)
        if n < 2 * early_quads:
            raw = dot_nn(prior_keys, q_from[:, cols])
            d_p = dot_nn(prior_keys[:, :LATENT], g_from[:, cols])
            return jnp.where(early, raw, own_s[:, cols]), jnp.where(early, d_p, own_d[:, cols])
        raw = dot_nn(all_keys, q_from[:, cols])
        d_p = dot_nn(all_keys[:, :LATENT], g_from[:, cols])
        return jnp.where(early, raw[:tok], raw[tok:]), jnp.where(early, d_p[:tok], d_p[tok:])

    def softmax_of(n, raw, d_p):
        heads = head_slots(n // 2)[2 * (n % 2) : 2 * (n % 2) + 2]
        squashed = jnp.tanh(raw * (SCALE / CAP))
        weights = jnp.where(allowed, jnp.exp2((CAP * LOG2_E) * squashed), 0.0)
        opened = jax.nn.sigmoid(jnp.concatenate([gate_t[pl.ds(h, 1), :] for h in heads], axis=1))
        inverse = 1.0 / jnp.sum(weights, axis=0, keepdims=True)
        mean = jnp.sum(weights * d_p, axis=0, keepdims=True) * inverse
        gate_grad = opened * (1.0 - opened) * mean
        for at, h in enumerate(heads):
            d_gate[pl.ds(h, 1), :] = gate_grad[:, at * tok : (at + 1) * tok]
        gated = weights * (inverse * opened)
        slope = gated * (d_p - mean) * (SCALE - SCALE * squashed * squashed)
        rows = pl.ds(n * 2 * tok, 2 * tok)
        d_raw[rows, :] = slope.astype(BF16).T
        d_val[rows, :] = gated.astype(BF16).T

    def unfolded(folded):
        return jnp.concatenate(
            [jnp.where(early_row, folded, nothing), jnp.where(early_row, nothing, folded)], axis=1
        )

    def add_up(n):
        q_from, g_from, cols = place(n)
        rows = pl.ds(n * 2 * tok, 2 * tok)
        slope = unfolded(d_raw[rows, :])
        both = jnp.concatenate([slope, unfolded(d_val[rows, :])], axis=0)
        left = jnp.concatenate([q_from[pl.ds(0, LATENT), cols], g_from[:, cols]], axis=1)
        total[pl.ds(0, LATENT), :] += dot_nn(left, both)
        total[pl.ds(LATENT, ROPE), :] += dot_nn(q_from[pl.ds(LATENT, ROPE), cols], slope)

    count = 2 * (early_quads + late_quads)
    raws = {}
    for n in range(count + 2):
        if n % 2 == 0 and n // 2 < late_quads:
            quad = n // 2
            turn(
                q_late[pl.ds(2 * quad * tok, 2 * tok), :], g_late[pl.ds(4 * quad * tok, 4 * tok), :],
                q_turned_late, g_turned_late, 4 * quad * tok, tok,
            )
        if n < count:
            raws[n] = scores_of(n)
        if 1 <= n <= count:
            softmax_of(n - 1, *raws.pop(n - 1))
        if n >= 2:
            add_up(n - 2)
    core = lax.axis_index("head") % 2
    half = WIDTH // 2
    mine = pl.ds(pl.multiple_of(core * half, 32), half)
    others = pl.ds(pl.multiple_of((1 - core) * half, 32), half)
    early_keep[...] = total[mine, :tok]
    own_keep[...] = total[mine, tok:]
    send[...] = total[others, :].astype(send.dtype)


def query_grads(first_quad, d_raw, prior_t, keys_t, after, *refs):
    out_hbm, done, stage, sems = refs[-4:]
    tok = d_raw.shape[1]
    quads = stage.shape[0] // (2 * tok)
    even_prior, odd_prior = padded_keys(prior_t[...])
    even_own, odd_own = padded_keys(keys_t[...])
    even = jnp.concatenate([even_prior, even_own], axis=0)
    odd = jnp.concatenate([odd_prior, odd_own], axis=0)
    middle = jnp.concatenate([even[:, LATENT:], odd[:, : 2 * ROPE]], axis=0)
    query_at = lax.broadcasted_iota(jnp.int32, (2 * tok, tok), 0) % tok
    key_at = lax.broadcasted_iota(jnp.int32, (2 * tok, tok), 1)
    early = key_at > query_at
    zero = jnp.zeros((2 * tok, tok), BF16)

    def unfolded(start):
        slope = d_raw[pl.ds(start, 2 * tok), :]
        return jnp.concatenate([jnp.where(early, slope, zero), jnp.where(early, zero, slope)], axis=1)

    copies = []
    for quad in range(quads):
        base = (first_quad + quad) * 4 * tok
        rows = pl.ds(quad * 2 * tok, 2 * tok)
        first = unfolded(base)
        second = unfolded(base + 2 * tok)
        stage[rows, pl.ds(0, LATENT)] = dot_nn(first, even[:, :LATENT]).astype(BF16)
        stage[rows, pl.ds(LATENT, 2 * ROPE)] = dot_nn(jnp.concatenate([first, second], axis=1), middle).astype(BF16)
        stage[rows, pl.ds(LATENT + 2 * ROPE, LATENT)] = dot_nn(second, odd[:, 2 * ROPE :]).astype(BF16)
        for n in range(2):
            pair = 2 * quad + n
            copies.append(
                pltpu.make_async_copy(
                    stage.at[pl.ds(pair * tok, tok), :],
                    out_hbm.at[:, pl.ds((2 * first_quad + pair) * PAIR, PAIR)],
                    sems.at[pair],
                )
            )
            copies[-1].start()
    for copy in copies:
        copy.wait()


def add_early(keep, other, out):
    out[...] = (keep[...] + other[:, : out.shape[1]].astype(F32)).astype(out.dtype)


def add_own(keep, other, returned, after, out):
    out[...] = (keep[...] + other[:, out.shape[1] :].astype(F32) + returned[...].astype(F32)).astype(out.dtype)


def add_halves(a, b, after, out):
    out[...] = (a[...].astype(F32) + b[...].astype(F32)).astype(out.dtype)


def shifted(value, axis, steps):
    count = lax.axis_size(axis)
    first, last = (max(0, -steps), min(count, count - steps))
    return lax.ppermute(value, axis, [(source, source + steps) for source in range(first, last)])


def shards(queries, latent, gate, d_out, segments):
    tok = latent.shape[0]
    heads = gate.shape[1]
    columns = heads * tok
    vmem = pl.BlockSpec(memory_space=pltpu.VMEM)
    hbm = pl.BlockSpec(memory_space=pl.ANY)
    params = pltpu.CompilerParams(vmem_limit_bytes=28 * 1024 * 1024)
    kept = pltpu.VMEM
    keys_t = latent.T
    gate_t = gate.T
    ids = segments.reshape(-1, tok)
    quads = heads // 4
    late = max(1, (quads * LATE) // 8)
    early = quads - late
    half = WIDTH // 2

    def cost(multiply_adds, moved):
        return pl.CostEstimate(flops=2 * multiply_adds, bytes_accessed=moved, transcendentals=0)

    prior_t = shifted(keys_t, "ctx", 1)
    kernel_in = [pltpu.with_memory_space_constraint(x, pltpu.HBM) for x in (queries, d_out, keys_t)]
    own_s, own_d, q_turned, g_turned, q_late, g_late, keys_t = pl.pallas_call(
        own_scores,
        out_shape=[
            kept((tok, 4 * early * tok), F32),
            kept((tok, 4 * early * tok), F32),
            kept((WIDTH, 4 * early * tok), BF16),
            kept((LATENT, 4 * early * tok), BF16),
            kept((2 * late * tok, PAIR), BF16),
            kept((4 * late * tok, LATENT), BF16),
            kept((WIDTH, tok), BF16),
        ],
        in_specs=[hbm] * 3,
        out_specs=[vmem] * 7,
        scratch_shapes=[
            pltpu.VMEM((2 * early * tok, PAIR), BF16),
            pltpu.VMEM((4 * early * tok, LATENT), BF16),
            pltpu.SemaphoreType.DMA((quads, 6)),
            pltpu.SemaphoreType.DMA((1,)),
        ],
        compiler_params=params,
        cost_estimate=cost(columns * tok * (PADDED + LATENT), queries.size * 2 + d_out.size * 2),
        name="own_scores",
    )(*kernel_in)
    d_raw, d_gate_t, early_keep, own_keep, send = pl.pallas_call(
        grads,
        out_shape=[
            kept((columns, tok), BF16),
            jax.ShapeDtypeStruct((heads, tok), F32),
            kept((half, tok), F32),
            kept((half, tok), F32),
            kept((half, 2 * tok), BF16),
        ],
        in_specs=[vmem] * 10,
        out_specs=[vmem] * 5,
        scratch_shapes=[
            pltpu.VMEM((WIDTH, 4 * late * tok), BF16),
            pltpu.VMEM((LATENT, 4 * late * tok), BF16),
            pltpu.VMEM((columns, tok), BF16),
            pltpu.VMEM((WIDTH, 2 * tok), F32),
        ],
        compiler_params=params,
        cost_estimate=cost(3 * columns * tok * (WIDTH + LATENT), 0),
        name="grads",
    )(own_s, own_d, q_turned, g_turned, q_late, g_late, prior_t, keys_t, gate_t, ids)
    group = lax.axis_size("head")

    def exchanged(value, step):
        return lax.ppermute(value, "head", [(i, i ^ step) for i in range(group)])

    def small(kernel, name, *operands):
        return pl.pallas_call(
            kernel,
            out_shape=kept((half, tok), BF16),
            in_specs=[vmem] * len(operands),
            out_specs=vmem,
            compiler_params=params,
            name=name,
        )(*operands)

    def query_part(first, count, after, *rest):
        return pl.pallas_call(
            functools.partial(query_grads, first),
            out_shape=[jax.ShapeDtypeStruct(queries.shape, queries.dtype), kept((8, 128), F32)],
            in_specs=[vmem] * 3 + [hbm] * (1 + len(rest)),
            out_specs=[hbm, vmem],
            scratch_shapes=[pltpu.VMEM((count * 2 * tok, PAIR), BF16), pltpu.SemaphoreType.DMA((2 * count,))],
            input_output_aliases={4: 0} if rest else {},
            compiler_params=params,
            cost_estimate=cost(count * 8 * tok * tok * PADDED, count * 4 * tok * PAIR),
            name="query_grads",
        )(d_raw, prior_t, keys_t, after, *rest)

    sent = exchanged(send, 1)
    returned = shifted(small(add_early, "add_early", early_keep, sent), "ctx", -1)
    cut = (quads + 1) // 2
    d_queries, done = query_part(0, cut, sent)
    total = small(add_own, "add_own", own_keep, sent, returned, done)
    d_queries, done = query_part(cut, quads - cut, total, d_queries)
    step = 2
    while step < group:
        total = small(add_halves, "add_halves", total, exchanged(total, step), done)
        step *= 2
    other = exchanged(total, 1)
    first = lax.axis_index("head") % 2 == 0
    d_latent_t = jnp.where(first, jnp.concatenate([total, other]), jnp.concatenate([other, total])).astype(F32)
    return d_queries, d_gate_t.T, d_latent_t.T


def solution(mesh):
    placed = (P("ctx", "head"), P("ctx", None), P("ctx", "head"), P("ctx", "head"), P())
    return jax.shard_map(
        shards,
        mesh=mesh,
        in_specs=placed,
        out_specs=(P("ctx", "head"), P("ctx", "head"), P("ctx", None)),
        check_vma=False,
    )
```

time: 88.9 us -> 30.9 us (0.35)
  local copies, waits for them, and re-layouts: 22 us -> 0.01 us
  matrix products: 21.6 us -> 0 us
  Pallas kernels: 0 us -> 14.8 us
  between operations: 14.2 us -> 0.74 us
  waiting for transfers between devices: 16.7 us -> 6.45 us
  blocking collectives: 6.07 us -> 0 us
  starting transfers between devices: 6.21 us -> 7.94 us
    dot_general x6 -> x0, matrix products: 21.6 us -> none  [the longest x1 5.13 us: local_grads(): jnp.einsum('qhd,kd->hqk', query_blk, all_keys, preferred_element_type=f32)]
    pallas_call x0 -> x7, Pallas kernels: none -> 14.8 us  [the longest x1 5.7 us: shards(): pl.pallas_call(grads, out_shape=[kept((columns, tok), BF16), jax.ShapeDty...]
    unnamed x18 -> x4, local copies, waits for them, and re-layouts: 14 us -> 0.01 us
    reduce_scatter x1 -> x0, waiting for transfers between devices: 10.8 us -> none  [shards(): lax.psum_scatter(owned_part + returned, 'head', scatter_dimension=1, tile...]
    convert_element_type x1 -> x0, local copies, waits for them, and re-layouts: 7.08 us -> none  [local_grads(): d_att = (opened[:, :, None] * cotangent).astype(jnp.bfloat16)]
    all_gather x1 -> x0, blocking collectives: 6.07 us -> none  [shards(): d_latent = lax.all_gather(column_share, 'head', axis=1, tiled=True)]
    ppermute x0 -> x3, waiting for transfers between devices: none -> 3.49 us  [exchanged(): return lax.ppermute(value, 'head', [(i, i ^ step) for i in range(group)])]
    ppermute x2, waiting for transfers between devices: 5.9 us -> 2.97 us  [shifted(): lax.ppermute(value, axis, [(source, source + steps) for source in range(f...]
  transfers between devices with their start and end apart: 3 -> 5, of which waited for: 2 -> 4; matrix products, arithmetic and copies ran while one was open for 29% -> 0% of each run, Pallas kernels for 0% -> 29%
where the time goes in v2:
time: 30.9 us; the launch traced here: 30.7 us
  Pallas kernels  14.8 us (48%)
  starting transfers between devices  7.94 us (26%)
  waiting for transfers between devices  6.45 us (21%)
  other arithmetic  0.74 us (2%)
  between operations  0.74 us (2%)
    ppermute x2, starting transfers between devices, shifted(): lax.ppermute(value, axis, [(source, source + steps) for source in range(f...  6.3 us
    pallas_call x1, Pallas kernels, shards(): pl.pallas_call(grads, out_shape=[kept((columns, tok), BF16), jax.ShapeDty...  5.7 us
    pallas_call x1, Pallas kernels, shards(): pl.pallas_call(own_scores, out_shape=[kept((tok, 4 * early * tok), F32),...  5.07 us
    pallas_call x2, Pallas kernels, query_part(): pl.pallas_call(functools.partial(query_grads, first), out_shape=[jax.Shap...  3.95 us
    ppermute x3, waiting for transfers between devices, exchanged(): return lax.ppermute(value, 'head', [(i, i ^ step) for i in range(group)])  3.49 us
    ppermute x2, waiting for transfers between devices, shifted(): lax.ppermute(value, axis, [(source, source + steps) for source in range(f...  2.97 us
    ppermute x3, starting transfers between devices, exchanged(): return lax.ppermute(value, 'head', [(i, i ^ step) for i in range(group)])  1.63 us
    transpose x1, other arithmetic, shards(): return (d_queries, d_gate_t.T, d_latent_t.T)  0.74 us
  transfers between devices with their start and end apart: 5, of which 4 were waited for; matrix products, arithmetic and copies ran while one was open for 0% of the time, Pallas kernels for 29%

profile of v2, /device:TPU:0, one launch (start us, length us, event | category | flops | bytes accessed | tf_op | source)
XLA Modules:
  0.0 30.7 jit_solution(12174982298440808482)
XLA Ops:
  0.6 0.0 copy-start
  0.6 0.0 copy-start.1
  0.7 5.0 %collective-permute-start = (bf16[576,128]{1,0:T(8,128)(2,1)}, bf16[576,128]{1,0:T(8,128)(2,1)S(1)}, u32[]{:S(2)}, u32[]{:S(2)}) collective-permute-start(bf16[576,128]{1,0:T(8,128)(2,1)} %bitcast.8), channel_id=1, source_target_pairs={{0,4},{4,8},{8,12},{12,16},{16,20},{20,24},{24,28},{1,5},{5,9},{9,... | collective-permute-start | bytes 442376 | tf_op jit(solution)/shard_map/ppermute | solution.py:256
  5.7 5.1 %own_scores.1 = (f32[128,2560]{1,0:T(8,128)S(1)}, f32[128,2560]{1,0:T(8,128)S(1)}, bf16[576,2560]{1,0:T(8,128)(2,1)S(1)}, bf16[512,2560]{1,0:T(8,128)(2,1)S(1)},...) custom-call(bf16[128,18432]{1,0:T(8,128)(2,1)} %q_hbm.1, ...), custom_call_target="tpu_custom_call" | custom-call | flops 1207959552 | bytes 8912896 | tf_op jit(solution)/shard_map/own_scores/pallas_call | solution.py:280
  10.7 0.0 collective-permute-done.prior_t
  10.8 0.0 copy-done
  10.8 0.0 copy-done.1
  10.8 5.7 %grads.1 = (bf16[4096,128]{1,0:T(8,128)(2,1)S(1)}, f32[32,128]{1,0:T(8,128)}, f32[288,128]{1,0:T(8,128)S(1)}, f32[288,128]{1,0:T(8,128)S(1)}, bf16[288,256]{1,0:T(8,128)(2,1)S(1)}) custom-call(f32[128,2560]{1,0:T(8,128)S(1)} %get-tuple-element.19.own_s, f32[128,2560]{1,0:T(8,128)S(1)} %get-tuple-element.20.own_d, ...), custom_call_target="tpu_custom_call" | custom-call | flops 3422552064 | tf_op jit(solution)/shard_map/grads/pallas_call | solution.py:303
  16.5 0.0 collective-permute-start.1
  16.5 1.4 %collective-permute-done.1.other.after = bf16[288,256]{1,0:T(8,128)(2,1)S(1)} collective-permute-done((bf16[288,256]{1,0:T(8,128)(2,1)S(1)}, bf16[288,256]{1,0:T(8,128)(2,1)S(1)}, u32[]{:S(2)}, u32[]{:S(2)}) %collective-permute-start.1) | collective-permute-done | bytes 147488 | tf_op jit(solution)/shard_map/ppermute | solution.py:327
  17.9 1.3 %collective-permute-start.2 = (bf16[288,128]{1,0:T(8,128)(2,1)S(1)}, bf16[288,128]{1,0:T(8,128)(2,1)S(1)}, u32[]{:S(2)}, u32[]{:S(2)}) collective-permute-start(bf16[288,128]{1,0:T(8,128)(2,1)S(1)} %add_early.1), channel_id=1, source_target_pairs={{4,0},{8,4},{12,8},{16,12},{20,16},{24,20},{28,24},{5,1},{9,5},{13... | collective-permute-start | bytes 221192 | tf_op jit(solution)/shard_map/ppermute | solution.py:256
  19.2 2.0 %query_grads.2 = (bf16[128,18432]{1,0:T(8,128)(2,1)}, f32[8,128]{1,0:T(8,128)S(1)}) custom-call(bf16[4096,128]{1,0:T(8,128)(2,1)S(1)} %get-tuple-element.26.d_raw, bf16[576,128]{1,0:T(8,128)(2,1)S(1)} %collective-permute-done.prior_t, bf16[576,128]{1,0:T(8,128)(2,1)S(1)} %get-tuple-element.25.keys_t, bf16[288,256]{1,0:T(8,128)(2,1)S(1)} %collective-permute-done.1.other.after), custom_call_target="tpu_custom_call" | custom-call | flops 671088640 | bytes 2359296 | tf_op jit(solution)/shard_map/query_grads/pallas_call | solution.py:340
  21.2 3.0 %collective-permute-done.2.returned = bf16[288,128]{1,0:T(8,128)(2,1)S(1)} collective-permute-done((bf16[288,128]{1,0:T(8,128)(2,1)S(1)}, bf16[288,128]{1,0:T(8,128)(2,1)S(1)}, u32[]{:S(2)}, u32[]{:S(2)}) %collective-permute-start.2) | collective-permute-done | bytes 73760 | tf_op jit(solution)/shard_map/ppermute | solution.py:256
  24.2 1.6 %collective-permute-start.3 = (bf16[288,128]{1,0:T(8,128)(2,1)S(1)}, bf16[288,128]{1,0:T(8,128)(2,1)S(1)}, u32[]{:S(2)}, u32[]{:S(2)}) collective-permute-start(bf16[288,128]{1,0:T(8,128)(2,1)S(1)} %add_own.1.after.a), channel_id=1, source_target_pairs={{0,2},{1,3},{2,0},{3,1},{4,6},{5,7},{6,4},{7,5},{8,10},{9,11},{10,... | collective-permute-start | bytes 221192 | tf_op jit(solution)/shard_map/ppermute | solution.py:327
  25.7 2.0 %query_grads.3 = (bf16[128,18432]{1,0:T(8,128)(2,1)}, f32[8,128]{1,0:T(8,128)S(1)}) custom-call(bf16[4096,128]{1,0:T(8,128)(2,1)S(1)} %get-tuple-element.26.d_raw, bf16[576,128]{1,0:T(8,128)(2,1)S(1)} %collective-permute-done.prior_t, bf16[576,128]{1,0:T(8,128)(2,1)S(1)} %get-tuple-element.25.keys_t, ...), custom_call_target="tpu_custom_call", output_to_operand_aliasing={{0}: (4, {})} | custom-call | flops 671088640 | bytes 2359296 | tf_op jit(solution)/shard_map/query_grads/pallas_call | solution.py:340
  27.7 0.9 %collective-permute-done.3.b = bf16[288,128]{1,0:T(8,128)(2,1)S(1)} collective-permute-done((bf16[288,128]{1,0:T(8,128)(2,1)S(1)}, bf16[288,128]{1,0:T(8,128)(2,1)S(1)}, u32[]{:S(2)}, u32[]{:S(2)}) %collective-permute-start.3) | collective-permute-done | bytes 73760 | tf_op jit(solution)/shard_map/ppermute | solution.py:327
  28.6 0.1 collective-permute-start.4
  28.7 1.2 %collective-permute-done.4 = bf16[288,128]{1,0:T(8,128)(2,1)S(1)} collective-permute-done((bf16[288,128]{1,0:T(8,128)(2,1)S(1)}, bf16[288,128]{1,0:T(8,128)(2,1)S(1)}, u32[]{:S(2)}, u32[]{:S(2)}) %collective-permute-start.4) | collective-permute-done | bytes 73760 | tf_op jit(solution)/shard_map/ppermute | solution.py:327
  29.9 0.7 %convert_bitcast_fusion = f32[128,576]{0,1:T(8,128)} fusion(bf16[288,128]{1,0:T(8,128)(2,1)S(1)} %collective-permute-done.4, bf16[288,128]{1,0:T(8,128)(2,1)S(1)} %add_halves.1, pred[]{:T(512)S(6)} %eq.5), kind=kLoop, calls=%fused_computation | loop fusion | flops 737280 | bytes 442369 | tf_op jit(solution)/shard_map/transpose | solution.py:365
  (3 shorter events, 0.1 us)
Async XLA Ops:
  0.6 10.1 %copy-start = (f32[128,32]{0,1:T(8,128)S(1)}, f32[128,32]{0,1:T(8,128)}, u32[]{:S(2)}) copy-start(f32[128,32]{0,1:T(8,128)} %param.7) | copy-start | bytes 49156
  0.6 10.1 %copy-start.1 = (s32[1024]{0:T(1024)S(1)}, s32[1024]{0:T(1024)}, u32[]{:S(2)}) copy-start(s32[1024]{0:T(1024)} %param.9) | copy-start | bytes 12292
  0.7 10.1 %collective-permute-start = (bf16[576,128]{1,0:T(8,128)(2,1)}, bf16[576,128]{1,0:T(8,128)(2,1)S(1)}, u32[]{:S(2)}, u32[]{:S(2)}) collective-permute-start(bf16[576,128]{1,0:T(8,128)(2,1)} %bitcast.8), channel_id=1, source_target_pairs={{0,4},{4,8},{8,12},{12,16},{16,20},{20,24},{24,28},{1,5},{5,9},{9,... | collective-permute-start | bytes 442376 | tf_op jit(solution)/shard_map/ppermute | solution.py:256
  16.5 1.4 %collective-permute-start.1 = (bf16[288,256]{1,0:T(8,128)(2,1)S(1)}, bf16[288,256]{1,0:T(8,128)(2,1)S(1)}, u32[]{:S(2)}, u32[]{:S(2)}) collective-permute-start(bf16[288,256]{1,0:T(8,128)(2,1)S(1)} %get-tuple-element.28), channel_id=1, source_target_pairs={{0,1},{1,0},{2,3},{3,2},{4,5},{5,4},{6,7},{7,6},{8,9},{9,8},{10,11... | collective-permute-start | bytes 442376 | tf_op jit(solution)/shard_map/ppermute | solution.py:327
  17.9 6.2 %collective-permute-start.2 = (bf16[288,128]{1,0:T(8,128)(2,1)S(1)}, bf16[288,128]{1,0:T(8,128)(2,1)S(1)}, u32[]{:S(2)}, u32[]{:S(2)}) collective-permute-start(bf16[288,128]{1,0:T(8,128)(2,1)S(1)} %add_early.1), channel_id=1, source_target_pairs={{4,0},{8,4},{12,8},{16,12},{20,16},{24,20},{28,24},{5,1},{9,5},{13... | collective-permute-start | bytes 221192 | tf_op jit(solution)/shard_map/ppermute | solution.py:256
  24.2 4.4 %collective-permute-start.3 = (bf16[288,128]{1,0:T(8,128)(2,1)S(1)}, bf16[288,128]{1,0:T(8,128)(2,1)S(1)}, u32[]{:S(2)}, u32[]{:S(2)}) collective-permute-start(bf16[288,128]{1,0:T(8,128)(2,1)S(1)} %add_own.1.after.a), channel_id=1, source_target_pairs={{0,2},{1,3},{2,0},{3,1},{4,6},{5,7},{6,4},{7,5},{8,10},{9,11},{10,... | collective-permute-start | bytes 221192 | tf_op jit(solution)/shard_map/ppermute | solution.py:327
  28.6 1.3 %collective-permute-start.4 = (bf16[288,128]{1,0:T(8,128)(2,1)S(1)}, bf16[288,128]{1,0:T(8,128)(2,1)S(1)}, u32[]{:S(2)}, u32[]{:S(2)}) collective-permute-start(bf16[288,128]{1,0:T(8,128)(2,1)S(1)} %add_halves.1), channel_id=1, source_target_pairs={{0,1},{1,0},{2,3},{3,2},{4,5},{5,4},{6,7},{7,6},{8,9},{9,8},{10,11... | collective-permute-start | bytes 221192 | tf_op jit(solution)/shard_map/ppermute | solution.py:327

commit v3 on v0

v3 whole, which is shorter than its diff:
```python
import functools

import jax
import jax.numpy as jnp
from jax import lax
from jax.experimental import pallas as pl
from jax.experimental.pallas import tpu as pltpu
from jax.sharding import PartitionSpec as P

LATENT = 512
ROPE = 64
WIDTH = LATENT + ROPE
PAIR = 2 * WIDTH
PADDED = LATENT + 2 * ROPE
SCALE = 192.0 ** (-0.5)
CAP = 20.0
LOG2_E = 1.4426950408889634
LANES = 128
TILE = 256
AHEAD = 3
EARLY = 4
BF16 = jnp.bfloat16
F32 = jnp.float32


def dot_nn(a, b):
    return lax.dot_general(a, b, (((1,), (0,)), ((), ())), preferred_element_type=F32)


def padded_keys(keys_t):
    spare = jnp.zeros((ROPE, keys_t.shape[1]), keys_t.dtype)
    even = jnp.concatenate([keys_t, spare], axis=0).T
    odd = jnp.concatenate([spare, keys_t], axis=0).T
    return even, odd


def latent_grad_t(even, odd, values):
    first = even + jnp.concatenate([values, jnp.zeros((values.shape[0], 2 * ROPE), F32)], axis=1)
    return first.T[:WIDTH] + odd.T[ROPE:]


def query_tile(q, block, odd):
    size = 2 * TILE * WIDTH // q.shape[1]
    rows, at = pl.ds(block * size, size), LATENT if odd else 0
    pairs = TILE // size
    return jnp.concatenate([q[rows, pl.ds(p * PAIR + at, PADDED)] for p in range(pairs)], axis=0)


def cotangent_tile(g, block, odd):
    size = 2 * TILE * LATENT // g.shape[1]
    rows = pl.ds(block * size, size)
    pairs = TILE // size
    return jnp.concatenate([g[rows, pl.ds((2 * p + odd) * LATENT, LATENT)] for p in range(pairs)], axis=0)


def turn(q, g, block, odd, q_turned, g_turned, start):
    cols = pl.ds(start, TILE)
    turned = query_tile(q, block, odd).T
    q_turned[:, cols] = turned[ROPE:] if odd else turned[:WIDTH]
    g_turned[:, cols] = cotangent_tile(g, block, odd).T


def spread(value, block, size):
    lane = lax.broadcasted_iota(jnp.int32, value.shape, 1)
    value = jnp.where(lane // size == block, value, jnp.zeros_like(value))
    shift = size
    while shift < value.shape[1]:
        value = value + pltpu.roll(value, shift, 1)
        shift *= 2
    return value


def head_of(shape, odd, part, size):
    return 2 * (part * (LANES // size) + lax.broadcasted_iota(jnp.int32, shape, 1) // size) + odd


def load(q_hbm, g_hbm, keys_hbm, q, g, q_turned, g_turned, keys_t, sems, key_sem):
    tok, heads = q.shape[0], g.shape[1] // LATENT
    size = 2 * TILE // heads
    blocks, early = tok // size, q_turned.shape[1] // (2 * TILE)
    keys_copy = pltpu.make_async_copy(keys_hbm, keys_t, key_sem.at[0])
    keys_copy.start()

    def copies(block):
        rows = pl.ds(block * size, size)
        return [
            pltpu.make_async_copy(s.at[rows, :], d.at[rows, :], sems.at[block, n])
            for n, (s, d) in enumerate(((q_hbm, q), (g_hbm, g)))
        ]

    for block in range(min(AHEAD, blocks)):
        for copy in copies(block):
            copy.start()
    for block in range(blocks):
        if block + AHEAD < blocks:
            for copy in copies(block + AHEAD):
                copy.start()
        for copy in copies(block):
            copy.wait()
        if block < early:
            for odd in (0, 1):
                turn(q, g, block, odd, q_turned, g_turned, (2 * block + odd) * TILE)
    keys_copy.wait()


def grads(
    q, g, q_turned, g_turned, prior_t, keys_t, gate_t, segments,
    d_raw, gate_rows, early_keep, own_keep, send,
    q_turned_late, g_turned_late, acc_even, acc_odd, acc_val, whole,
):
    tok, heads = gate_t.shape[1], gate_t.shape[0]
    size = 2 * TILE // heads
    window = tok + size
    blocks, early = tok // size, q_turned.shape[1] // (2 * TILE)
    shard = lax.axis_index("ctx")
    keys = jnp.concatenate([prior_t[...].T, keys_t[...].T], axis=0)
    row_own = segments[pl.ds(shard, 1), :]
    row_prior = segments[pl.ds(jnp.maximum(shard - 1, 0), 1), :]
    key_segment = jnp.concatenate(
        [jnp.broadcast_to(row_prior, (tok, tok)).T, jnp.broadcast_to(row_own, (tok, tok)).T], axis=0
    )
    for acc in (acc_even, acc_odd, acc_val):
        acc[...] = jnp.zeros_like(acc)

    def keys_of(block):
        return pl.ds(block * size, window)

    def allowed_in(block):
        key_at = block * size + lax.broadcasted_iota(jnp.int32, (window, tok), 0)
        query_at = block * size + lax.broadcasted_iota(jnp.int32, (window, tok), 1) % size
        query_segment = spread(jnp.broadcast_to(row_own, (8, tok)), block, size)[:1]
        same = key_segment[block * size : block * size + window] == query_segment
        allowed = same & (key_at - tok <= query_at) & ((key_at >= tok) | (shard > 0))
        return jnp.concatenate([allowed, allowed], axis=1)

    def gates_of(block, odd):
        spread_gate = spread(gate_t[...], block, size)
        head = lax.broadcasted_iota(jnp.int32, spread_gate.shape, 0)
        return jnp.concatenate(
            [
                jnp.sum(
                    jnp.where(head == head_of(spread_gate.shape, odd, part, size), spread_gate, 0.0),
                    axis=0,
                    keepdims=True,
                )
                for part in range(TILE // LANES)
            ],
            axis=1,
        )

    def scores_of(n):
        block = n // 2
        if block < early:
            q_from, g_from, cols = q_turned, g_turned, pl.ds(n * TILE, TILE)
        else:
            q_from, g_from, cols = q_turned_late, g_turned_late, pl.ds((n - 2 * early) * TILE, TILE)
        held = keys[block * size : block * size + window]
        return dot_nn(held, q_from[:, cols]), dot_nn(held[:, :LATENT], g_from[:, cols])

    def softmax_of(n, raw, d_p, allowed):
        squashed = jnp.tanh(raw * (SCALE / CAP))
        weights = jnp.where(allowed, jnp.exp2((CAP * LOG2_E) * squashed), 0.0)
        opened = jax.nn.sigmoid(gates_of(n // 2, n % 2))
        inverse = 1.0 / jnp.sum(weights, axis=0, keepdims=True)
        mean = jnp.sum(weights * d_p, axis=0, keepdims=True) * inverse
        gate_rows[pl.ds(n, 1), :] = opened * (1.0 - opened) * mean
        gated = weights * (inverse * opened)
        slope = gated * (d_p - mean) * (SCALE - SCALE * squashed * squashed)
        d_raw[pl.ds(n * window, window), :] = slope.astype(BF16)
        return gated.astype(BF16)

    def add_up(n, gated):
        block, odd = n // 2, n % 2
        acc = acc_odd if odd else acc_even
        acc[keys_of(block), :] += dot_nn(d_raw[pl.ds(n * window, window), :], query_tile(q, block, odd))
        acc_val[keys_of(block), :] += dot_nn(gated, cotangent_tile(g, block, odd))

    count = 2 * blocks
    raws, gateds = {}, {}
    turned = 2 * early
    for n in range(count + 2):
        while turned < min(count, n + 2):
            turn(q, g, turned // 2, turned % 2, q_turned_late, g_turned_late, (turned - 2 * early) * TILE)
            turned += 1
        if n < count:
            raws[n] = scores_of(n)
        if 1 <= n <= count:
            if n % 2:
                allowed = allowed_in((n - 1) // 2)
            gateds[n - 1] = softmax_of(n - 1, *raws.pop(n - 1), allowed)
        if n >= 2:
            add_up(n - 2, gateds.pop(n - 2))
    whole[...] = latent_grad_t(acc_even[...], acc_odd[...], acc_val[...])
    core = lax.axis_index("head") % 2
    half = WIDTH // 2
    mine = pl.ds(pl.multiple_of(core * half, 32), half)
    others = pl.ds(pl.multiple_of((1 - core) * half, 32), half)
    early_keep[...] = whole[mine, :tok]
    own_keep[...] = whole[mine, tok:]
    send[...] = whole[others, :].astype(send.dtype)


def query_grads(first_block, d_raw, prior_t, keys_t, gate_rows, after, *refs):
    stage, sems = refs[-2:]
    if first_block == 0:
        out_hbm, done, d_gate = refs[-5:-2]
    else:
        out_hbm, done = refs[-4:-2]
    tok = keys_t.shape[1]
    heads = stage.shape[1] // WIDTH
    size = 2 * TILE // heads
    window = tok + size
    pairs = TILE // size
    even_prior, odd_prior = padded_keys(prior_t[...])
    even_own, odd_own = padded_keys(keys_t[...])
    even = jnp.concatenate([even_prior, even_own], axis=0)
    odd = jnp.concatenate([odd_prior, odd_own], axis=0)
    copies = []
    for at in range(stage.shape[0] // size):
        block = first_block + at
        low, high = block * size, block * size + window
        slopes = [d_raw[pl.ds((2 * block + n) * window, window), :].T for n in range(2)]
        middle = jnp.concatenate([even[low:high, LATENT:], odd[low:high, : 2 * ROPE]], axis=0)
        for column, part in (
            (0, dot_nn(slopes[0], even[low:high, :LATENT])),
            (LATENT, dot_nn(jnp.concatenate(slopes, axis=1), middle)),
            (LATENT + 2 * ROPE, dot_nn(slopes[1], odd[low:high, 2 * ROPE :])),
        ):
            part = part.astype(BF16)
            for p in range(pairs):
                stage[pl.ds(at * size, size), pl.ds(p * PAIR + column, part.shape[1])] = part[
                    p * size : (p + 1) * size
                ]
        copies.append(
            pltpu.make_async_copy(
                stage.at[pl.ds(at * size, size), :], out_hbm.at[pl.ds(low, size), :], sems.at[at]
            )
        )
        copies[-1].start()
    if first_block == 0:
        shape = d_gate.shape
        head = lax.broadcasted_iota(jnp.int32, shape, 0)
        lane = lax.broadcasted_iota(jnp.int32, shape, 1)
        found = jnp.zeros(shape, F32)
        for block in range(tok // size):
            value = jnp.zeros(shape, F32)
            for n in range(2):
                row = gate_rows[pl.ds(2 * block + n, 1), :]
                for part in range(TILE // LANES):
                    held = jnp.broadcast_to(row[:, part * LANES : (part + 1) * LANES], shape)
                    value = jnp.where(head == head_of(shape, n, part, size), held, value)
            shift = size
            while shift < tok:
                value = value + pltpu.roll(value, shift, 1)
                shift *= 2
            found = jnp.where(lane // size == block, value, found)
        d_gate[...] = found
    for copy in copies:
        copy.wait()
    done[...] = jnp.zeros_like(done)


def add_early(keep, other, out):
    out[...] = (keep[...] + other[:, : out.shape[1]].astype(F32)).astype(out.dtype)


def add_own(keep, other, returned, after, out):
    out[...] = (keep[...] + other[:, out.shape[1] :].astype(F32) + returned[...].astype(F32)).astype(out.dtype)


def add_halves(a, b, after, out):
    out[...] = (a[...].astype(F32) + b[...].astype(F32)).astype(out.dtype)


def shifted(value, axis, steps):
    count = lax.axis_size(axis)
    first, last = (max(0, -steps), min(count, count - steps))
    return lax.ppermute(value, axis, [(source, source + steps) for source in range(first, last)])


def shards(queries, latent, gate, d_out, segments):
    tok = latent.shape[0]
    heads = gate.shape[1]
    size = 2 * TILE // heads
    window = tok + size
    blocks = tok // size
    early = max(1, blocks * EARLY // 8)
    half = WIDTH // 2
    columns = heads * tok
    vmem = pl.BlockSpec(memory_space=pltpu.VMEM)
    hbm = pl.BlockSpec(memory_space=pl.ANY)
    params = pltpu.CompilerParams(vmem_limit_bytes=28 * 1024 * 1024)
    kept = pltpu.VMEM
    keys_t = latent.T
    gate_t = gate.T
    ids = segments.reshape(-1, tok)

    def cost(multiply_adds, moved):
        return pl.CostEstimate(flops=2 * multiply_adds, bytes_accessed=moved, transcendentals=0)

    prior_t = shifted(keys_t, "ctx", 1)
    q, g, q_turned, g_turned, keys_t = pl.pallas_call(
        load,
        out_shape=[
            kept(queries.shape, BF16),
            kept(d_out.shape, BF16),
            kept((WIDTH, 2 * early * TILE), BF16),
            kept((LATENT, 2 * early * TILE), BF16),
            kept((WIDTH, tok), BF16),
        ],
        in_specs=[hbm] * 3,
        out_specs=[vmem] * 5,
        scratch_shapes=[pltpu.SemaphoreType.DMA((blocks, 2)), pltpu.SemaphoreType.DMA((1,))],
        compiler_params=params,
        cost_estimate=cost(0, queries.size * 2 + d_out.size * 2),
        name="load",
    )(*[pltpu.with_memory_space_constraint(x, pltpu.HBM) for x in (queries, d_out, keys_t)])
    d_raw, gate_rows, early_keep, own_keep, send = pl.pallas_call(
        grads,
        out_shape=[
            kept((2 * blocks * window, TILE), BF16),
            kept((2 * blocks, TILE), F32),
            kept((half, tok), F32),
            kept((half, tok), F32),
            kept((half, 2 * tok), BF16),
        ],
        in_specs=[vmem] * 8,
        out_specs=[vmem] * 5,
        scratch_shapes=[
            pltpu.VMEM((WIDTH, 2 * (blocks - early) * TILE), BF16),
            pltpu.VMEM((LATENT, 2 * (blocks - early) * TILE), BF16),
            pltpu.VMEM((2 * tok, PADDED), F32),
            pltpu.VMEM((2 * tok, PADDED), F32),
            pltpu.VMEM((2 * tok, LATENT), F32),
            pltpu.VMEM((WIDTH, 2 * tok), F32),
        ],
        compiler_params=params,
        cost_estimate=cost(2 * columns * window * (WIDTH + LATENT), 0),
        name="grads",
    )(q, g, q_turned, g_turned, prior_t, keys_t, gate_t, ids)
    group = lax.axis_size("head")

    def exchanged(value, step):
        return lax.ppermute(value, "head", [(i, i ^ step) for i in range(group)])

    def small(kernel, name, *operands):
        return pl.pallas_call(
            kernel,
            out_shape=kept((half, tok), BF16),
            in_specs=[vmem] * len(operands),
            out_specs=vmem,
            compiler_params=params,
            name=name,
        )(*operands)

    def query_part(first, count, after, *rest):
        d_gate = [] if rest else [jax.ShapeDtypeStruct((heads, tok), F32)]
        return pl.pallas_call(
            functools.partial(query_grads, first),
            out_shape=[jax.ShapeDtypeStruct(queries.shape, queries.dtype), kept((8, 128), F32)] + d_gate,
            in_specs=[vmem] * 4 + [hbm] * (1 + len(rest)),
            out_specs=[hbm, vmem] + [vmem] * len(d_gate),
            scratch_shapes=[
                pltpu.VMEM((count * size, queries.shape[1]), BF16),
                pltpu.SemaphoreType.DMA((count,)),
            ],
            input_output_aliases={5: 0} if rest else {},
            compiler_params=params,
            cost_estimate=cost(count * 2 * TILE * window * PADDED, count * size * queries.shape[1] * 2),
            name="query_grads",
        )(d_raw, prior_t, keys_t, gate_rows, after, *rest)

    sent = exchanged(send, 1)
    returned = shifted(small(add_early, "add_early", early_keep, sent), "ctx", -1)
    cut = (blocks + 1) // 2
    d_queries, done, d_gate_t = query_part(0, cut, sent)
    total = small(add_own, "add_own", own_keep, sent, returned, done)
    d_queries, done = query_part(cut, blocks - cut, total, d_queries)
    step = 2
    while step < group:
        total = small(add_halves, "add_halves", total, exchanged(total, step), done)
        step *= 2
    other = exchanged(total, 1)
    first = lax.axis_index("head") % 2 == 0
    d_latent_t = jnp.where(first, jnp.concatenate([total, other]), jnp.concatenate([other, total])).astype(F32)
    return d_queries, d_gate_t.T, d_latent_t.T


def solution(mesh):
    placed = (P("ctx", "head"), P("ctx", None), P("ctx", "head"), P("ctx", "head"), P())
    return jax.shard_map(
        shards,
        mesh=mesh,
        in_specs=placed,
        out_specs=(P("ctx", "head"), P("ctx", "head"), P("ctx", None)),
        check_vma=False,
    )
```

time: 88.9 us -> 29.2 us (0.33)
  local copies, waits for them, and re-layouts: 22 us -> 0.01 us
  matrix products: 21.6 us -> 0 us
  Pallas kernels: 0 us -> 13.8 us
  between operations: 14.2 us -> 0.75 us
  waiting for transfers between devices: 16.7 us -> 5.71 us
  blocking collectives: 6.07 us -> 0 us
  starting transfers between devices: 6.21 us -> 7.99 us
    dot_general x6 -> x0, matrix products: 21.6 us -> none  [the longest x1 5.13 us: local_grads(): jnp.einsum('qhd,kd->hqk', query_blk, all_keys, preferred_element_type=f32)]
    unnamed x18 -> x4, local copies, waits for them, and re-layouts: 14 us -> 0.01 us
    pallas_call x0 -> x7, Pallas kernels: none -> 13.8 us  [the longest x1 4.85 us: shards(): pl.pallas_call(grads, out_shape=[kept((2 * blocks * window, TILE), BF16),...]
    reduce_scatter x1 -> x0, waiting for transfers between devices: 10.8 us -> none  [shards(): lax.psum_scatter(owned_part + returned, 'head', scatter_dimension=1, tile...]
    convert_element_type x1 -> x0, local copies, waits for them, and re-layouts: 7.08 us -> none  [local_grads(): d_att = (opened[:, :, None] * cotangent).astype(jnp.bfloat16)]
    all_gather x1 -> x0, blocking collectives: 6.07 us -> none  [shards(): d_latent = lax.all_gather(column_share, 'head', axis=1, tiled=True)]
    ppermute x2, waiting for transfers between devices: 5.9 us -> 2.3 us  [shifted(): lax.ppermute(value, axis, [(source, source + steps) for source in range(f...]
    ppermute x0 -> x3, waiting for transfers between devices: none -> 3.41 us  [exchanged(): return lax.ppermute(value, 'head', [(i, i ^ step) for i in range(group)])]
  transfers between devices with their start and end apart: 3 -> 5, of which waited for: 2 -> 4; matrix products, arithmetic and copies ran while one was open for 29% -> 0% of each run, Pallas kernels for 0% -> 31%
where the time goes in v3:
time: 29.2 us; the launch traced here: 29 us
  Pallas kernels  13.8 us (47%)
  starting transfers between devices  7.99 us (27%)
  waiting for transfers between devices  5.71 us (20%)
  between operations  0.75 us (3%)
  other arithmetic  0.74 us (3%)
    ppermute x2, starting transfers between devices, shifted(): lax.ppermute(value, axis, [(source, source + steps) for source in range(f...  6.3 us
    pallas_call x1, Pallas kernels, shards(): pl.pallas_call(grads, out_shape=[kept((2 * blocks * window, TILE), BF16),...  4.85 us
    pallas_call x2, Pallas kernels, query_part(): pl.pallas_call(functools.partial(query_grads, first), out_shape=[jax.Shap...  4.69 us
    pallas_call x1, Pallas kernels, shards(): pl.pallas_call(load, out_shape=[kept(queries.shape, BF16), kept(d_out.sha...  4.17 us
    ppermute x3, waiting for transfers between devices, exchanged(): return lax.ppermute(value, 'head', [(i, i ^ step) for i in range(group)])  3.41 us
    ppermute x2, waiting for transfers between devices, shifted(): lax.ppermute(value, axis, [(source, source + steps) for source in range(f...  2.3 us
    ppermute x3, starting transfers between devices, exchanged(): return lax.ppermute(value, 'head', [(i, i ^ step) for i in range(group)])  1.69 us
    transpose x1, other arithmetic, shards(): return (d_queries, d_gate_t.T, d_latent_t.T)  0.74 us
  transfers between devices with their start and end apart: 5, of which 4 were waited for; matrix products, arithmetic and copies ran while one was open for 0% of the time, Pallas kernels for 31%

profile of v3, /device:TPU:0, one launch (start us, length us, event | category | flops | bytes accessed | tf_op | source)
XLA Modules:
  0.0 29.0 jit_solution(13078202050497332151)
XLA Ops:
  0.6 0.0 copy-start
  0.6 0.0 copy-start.1
  0.7 5.0 %collective-permute-start = (bf16[576,128]{1,0:T(8,128)(2,1)}, bf16[576,128]{1,0:T(8,128)(2,1)S(1)}, u32[]{:S(2)}, u32[]{:S(2)}) collective-permute-start(bf16[576,128]{1,0:T(8,128)(2,1)} %bitcast.8), channel_id=1, source_target_pairs={{0,4},{4,8},{8,12},{12,16},{16,20},{20,24},{24,28},{1,5},{5,9},{9,... | collective-permute-start | bytes 442376 | tf_op jit(solution)/shard_map/ppermute | solution.py:278
  5.7 4.2 %load.1 = (bf16[128,18432]{1,0:T(8,128)(2,1)S(1)}, bf16[128,16384]{1,0:T(8,128)(2,1)S(1)}, bf16[576,2048]{1,0:T(8,128)(2,1)S(1)}, bf16[512,2048]{1,0:T(8,128)(2,1)S(1)}, bf16[576,128]{1,0:T(8,128)(2,1)S(1)}) custom-call(bf16[128,18432]{1,0:T(8,128)(2,1)} %q_hbm.1, bf16[128,16384]{1,0:T(8,128)(2,1)} %g_hbm.1, bf16[576,128]{1,0:T(8,128)(2,1)} %bitcast.9), custom_call_target="tpu_custom_call" | custom-call | bytes 8912896 | tf_op jit(solution)/shard_map/load/pallas_call | solution.py:302
  9.9 0.0 collective-permute-done.prior_t
  9.9 0.0 copy-done
  9.9 0.0 copy-done.1
  9.9 4.8 %grads.1 = (bf16[2304,256]{1,0:T(8,128)(2,1)S(1)}, f32[16,256]{1,0:T(8,128)S(1)}, f32[288,128]{1,0:T(8,128)S(1)}, f32[288,128]{1,0:T(8,128)S(1)}, bf16[288,256]{1,0:T(8,128)(2,1)S(1)}) custom-call(bf16[128,18432]{1,0:T(8,128)(2,1)S(1)} %get-tuple-element.18.q, bf16[128,16384]{1,0:T(8,128)(2,1)S(1)} %get-tuple-element.19.g, ...), custom_call_target="tpu_custom_call" | custom-call | flops 2566914048 | tf_op jit(solution)/shard_map/grads/pallas_call | solution.py:318
  14.7 0.1 collective-permute-start.1
  14.8 1.4 %collective-permute-done.1.other.after = bf16[288,256]{1,0:T(8,128)(2,1)S(1)} collective-permute-done((bf16[288,256]{1,0:T(8,128)(2,1)S(1)}, bf16[288,256]{1,0:T(8,128)(2,1)S(1)}, u32[]{:S(2)}, u32[]{:S(2)}) %collective-permute-start.1) | collective-permute-done | bytes 147488 | tf_op jit(solution)/shard_map/ppermute | solution.py:344
  16.2 1.3 %collective-permute-start.2 = (bf16[288,128]{1,0:T(8,128)(2,1)S(1)}, bf16[288,128]{1,0:T(8,128)(2,1)S(1)}, u32[]{:S(2)}, u32[]{:S(2)}) collective-permute-start(bf16[288,128]{1,0:T(8,128)(2,1)S(1)} %add_early.1), channel_id=1, source_target_pairs={{4,0},{8,4},{12,8},{16,12},{20,16},{24,20},{28,24},{5,1},{9,5},{13... | collective-permute-start | bytes 221192 | tf_op jit(solution)/shard_map/ppermute | solution.py:278
  17.5 2.6 %query_grads.2 = (bf16[128,18432]{1,0:T(8,128)(2,1)}, f32[8,128]{1,0:T(8,128)S(1)}, f32[32,128]{1,0:T(8,128)}) custom-call(bf16[2304,256]{1,0:T(8,128)(2,1)S(1)} %get-tuple-element.23.d_raw, bf16[576,128]{1,0:T(8,128)(2,1)S(1)} %collective-permute-done.prior_t, bf16[576,128]{1,0:T(8,128)(2,1)S(1)} %get-tuple-element.22.keys_t, ...), custom_call_target="tpu_custom_call" | custom-call | flops 377487360 | bytes 2359296 | tf_op jit(solution)/shard_map/query_grads/pallas_call | solution.py:358
  20.1 2.3 %collective-permute-done.2.returned = bf16[288,128]{1,0:T(8,128)(2,1)S(1)} collective-permute-done((bf16[288,128]{1,0:T(8,128)(2,1)S(1)}, bf16[288,128]{1,0:T(8,128)(2,1)S(1)}, u32[]{:S(2)}, u32[]{:S(2)}) %collective-permute-start.2) | collective-permute-done | bytes 73760 | tf_op jit(solution)/shard_map/ppermute | solution.py:278
  22.5 1.5 %collective-permute-start.3 = (bf16[288,128]{1,0:T(8,128)(2,1)S(1)}, bf16[288,128]{1,0:T(8,128)(2,1)S(1)}, u32[]{:S(2)}, u32[]{:S(2)}) collective-permute-start(bf16[288,128]{1,0:T(8,128)(2,1)S(1)} %add_own.1.after.a), channel_id=1, source_target_pairs={{0,2},{1,3},{2,0},{3,1},{4,6},{5,7},{6,4},{7,5},{8,10},{9,11},{10,... | collective-permute-start | bytes 221192 | tf_op jit(solution)/shard_map/ppermute | solution.py:344
  24.0 2.0 %query_grads.3 = (bf16[128,18432]{1,0:T(8,128)(2,1)}, f32[8,128]{1,0:T(8,128)S(1)}) custom-call(bf16[2304,256]{1,0:T(8,128)(2,1)S(1)} %get-tuple-element.23.d_raw, bf16[576,128]{1,0:T(8,128)(2,1)S(1)} %collective-permute-done.prior_t, bf16[576,128]{1,0:T(8,128)(2,1)S(1)} %get-tuple-element.22.keys_t, ...), custom_call_target="tpu_custom_call", output_to_operand_aliasing={{0}: (5, {})} | custom-call | flops 377487360 | bytes 2359296 | tf_op jit(solution)/shard_map/query_grads/pallas_call | solution.py:358
  26.1 0.8 %collective-permute-done.3.b = bf16[288,128]{1,0:T(8,128)(2,1)S(1)} collective-permute-done((bf16[288,128]{1,0:T(8,128)(2,1)S(1)}, bf16[288,128]{1,0:T(8,128)(2,1)S(1)}, u32[]{:S(2)}, u32[]{:S(2)}) %collective-permute-start.3) | collective-permute-done | bytes 73760 | tf_op jit(solution)/shard_map/ppermute | solution.py:344
  26.9 0.1 collective-permute-start.4
  27.0 1.2 %collective-permute-done.4 = bf16[288,128]{1,0:T(8,128)(2,1)S(1)} collective-permute-done((bf16[288,128]{1,0:T(8,128)(2,1)S(1)}, bf16[288,128]{1,0:T(8,128)(2,1)S(1)}, u32[]{:S(2)}, u32[]{:S(2)}) %collective-permute-start.4) | collective-permute-done | bytes 73760 | tf_op jit(solution)/shard_map/ppermute | solution.py:344
  28.2 0.7 %convert_bitcast_fusion = f32[128,576]{0,1:T(8,128)} fusion(bf16[288,128]{1,0:T(8,128)(2,1)S(1)} %collective-permute-done.4, bf16[288,128]{1,0:T(8,128)(2,1)S(1)} %add_halves.1, pred[]{:T(512)S(6)} %eq.5), kind=kLoop, calls=%fused_computation | loop fusion | flops 737280 | bytes 442369 | tf_op jit(solution)/shard_map/transpose | solution.py:386
  (3 shorter events, 0.1 us)
Async XLA Ops:
  0.6 9.2 %copy-start = (f32[128,32]{0,1:T(8,128)S(1)}, f32[128,32]{0,1:T(8,128)}, u32[]{:S(2)}) copy-start(f32[128,32]{0,1:T(8,128)} %param.7) | copy-start | bytes 49156
  0.6 9.2 %copy-start.1 = (s32[1024]{0:T(1024)S(1)}, s32[1024]{0:T(1024)}, u32[]{:S(2)}) copy-start(s32[1024]{0:T(1024)} %param.9) | copy-start | bytes 12292
  0.7 9.2 %collective-permute-start = (bf16[576,128]{1,0:T(8,128)(2,1)}, bf16[576,128]{1,0:T(8,128)(2,1)S(1)}, u32[]{:S(2)}, u32[]{:S(2)}) collective-permute-start(bf16[576,128]{1,0:T(8,128)(2,1)} %bitcast.8), channel_id=1, source_target_pairs={{0,4},{4,8},{8,12},{12,16},{16,20},{20,24},{24,28},{1,5},{5,9},{9,... | collective-permute-start | bytes 442376 | tf_op jit(solution)/shard_map/ppermute | solution.py:278
  14.7 1.4 %collective-permute-start.1 = (bf16[288,256]{1,0:T(8,128)(2,1)S(1)}, bf16[288,256]{1,0:T(8,128)(2,1)S(1)}, u32[]{:S(2)}, u32[]{:S(2)}) collective-permute-start(bf16[288,256]{1,0:T(8,128)(2,1)S(1)} %get-tuple-element.26), channel_id=1, source_target_pairs={{0,1},{1,0},{2,3},{3,2},{4,5},{5,4},{6,7},{7,6},{8,9},{9,8},{10,11... | collective-permute-start | bytes 442376 | tf_op jit(solution)/shard_map/ppermute | solution.py:344
  16.2 6.2 %collective-permute-start.2 = (bf16[288,128]{1,0:T(8,128)(2,1)S(1)}, bf16[288,128]{1,0:T(8,128)(2,1)S(1)}, u32[]{:S(2)}, u32[]{:S(2)}) collective-permute-start(bf16[288,128]{1,0:T(8,128)(2,1)S(1)} %add_early.1), channel_id=1, source_target_pairs={{4,0},{8,4},{12,8},{16,12},{20,16},{24,20},{28,24},{5,1},{9,5},{13... | collective-permute-start | bytes 221192 | tf_op jit(solution)/shard_map/ppermute | solution.py:278
  22.5 4.4 %collective-permute-start.3 = (bf16[288,128]{1,0:T(8,128)(2,1)S(1)}, bf16[288,128]{1,0:T(8,128)(2,1)S(1)}, u32[]{:S(2)}, u32[]{:S(2)}) collective-permute-start(bf16[288,128]{1,0:T(8,128)(2,1)S(1)} %add_own.1.after.a), channel_id=1, source_target_pairs={{0,2},{1,3},{2,0},{3,1},{4,6},{5,7},{6,4},{7,5},{8,10},{9,11},{10,... | collective-permute-start | bytes 221192 | tf_op jit(solution)/shard_map/ppermute | solution.py:344
  26.9 1.3 %collective-permute-start.4 = (bf16[288,128]{1,0:T(8,128)(2,1)S(1)}, bf16[288,128]{1,0:T(8,128)(2,1)S(1)}, u32[]{:S(2)}, u32[]{:S(2)}) collective-permute-start(bf16[288,128]{1,0:T(8,128)(2,1)S(1)} %add_halves.1), channel_id=1, source_target_pairs={{0,1},{1,0},{2,3},{3,2},{4,5},{5,4},{6,7},{7,6},{8,9},{9,8},{10,11... | collective-permute-start | bytes 221192 | tf_op jit(solution)/shard_map/ppermute | solution.py:344

commit v4 on v3

--- a/solution.py
+++ b/solution.py
@@ -17,8 +17,8 @@
 LOG2_E = 1.4426950408889634
 LANES = 128
 TILE = 256
-AHEAD = 3
-EARLY = 4
+AHEAD = 8
+EARLY = 7
 BF16 = jnp.bfloat16
 F32 = jnp.float32
 
@@ -131,7 +131,7 @@
         query_segment = spread(jnp.broadcast_to(row_own, (8, tok)), block, size)[:1]
         same = key_segment[block * size : block * size + window] == query_segment
         allowed = same & (key_at - tok <= query_at) & ((key_at >= tok) | (shard > 0))
-        return jnp.concatenate([allowed, allowed], axis=1)
+        return allowed
 
     def gates_of(block, odd):
         spread_gate = spread(gate_t[...], block, size)
@@ -158,16 +158,21 @@
         return dot_nn(held, q_from[:, cols]), dot_nn(held[:, :LATENT], g_from[:, cols])
 
     def softmax_of(n, raw, d_p, allowed):
-        squashed = jnp.tanh(raw * (SCALE / CAP))
-        weights = jnp.where(allowed, jnp.exp2((CAP * LOG2_E) * squashed), 0.0)
-        opened = jax.nn.sigmoid(gates_of(n // 2, n % 2))
-        inverse = 1.0 / jnp.sum(weights, axis=0, keepdims=True)
-        mean = jnp.sum(weights * d_p, axis=0, keepdims=True) * inverse
-        gate_rows[pl.ds(n, 1), :] = opened * (1.0 - opened) * mean
-        gated = weights * (inverse * opened)
-        slope = gated * (d_p - mean) * (SCALE - SCALE * squashed * squashed)
-        d_raw[pl.ds(n * window, window), :] = slope.astype(BF16)
-        return gated.astype(BF16)
+        gate = gates_of(n // 2, n % 2)
+        gateds = []
+        for part in range(TILE // LANES):
+            lanes = slice(part * LANES, (part + 1) * LANES)
+            squashed = jnp.tanh(raw[:, lanes] * (SCALE / CAP))
+            weights = jnp.where(allowed, jnp.exp2((CAP * LOG2_E) * squashed), 0.0)
+            opened = jax.nn.sigmoid(gate[:, lanes])
+            inverse = 1.0 / jnp.sum(weights, axis=0, keepdims=True)
+            mean = jnp.sum(weights * d_p[:, lanes], axis=0, keepdims=True) * inverse
+            gate_rows[pl.ds(n, 1), pl.ds(part * LANES, LANES)] = opened * (1.0 - opened) * mean
+            gated = weights * (inverse * opened)
+            slope = gated * (d_p[:, lanes] - mean) * (SCALE - SCALE * squashed * squashed)
+            d_raw[pl.ds(n * window, window), pl.ds(part * LANES, LANES)] = slope.astype(BF16)
+            gateds.append(gated.astype(BF16))
+        return jnp.concatenate(gateds, axis=1)
 
     def add_up(n, gated):
         block, odd = n // 2, n % 2
@@ -190,14 +195,16 @@
             gateds[n - 1] = softmax_of(n - 1, *raws.pop(n - 1), allowed)
         if n >= 2:
             add_up(n - 2, gateds.pop(n - 2))
-    whole[...] = latent_grad_t(acc_even[...], acc_odd[...], acc_val[...])
+    odd_moved = pltpu.roll(acc_odd[...], PADDED - ROPE, 1)
+    summed = acc_even[...] + odd_moved + jnp.concatenate([acc_val[...], jnp.zeros((2 * tok, 2 * ROPE), F32)], axis=1)
+    whole[...] = summed.astype(BF16).T[:WIDTH]
     core = lax.axis_index("head") % 2
     half = WIDTH // 2
     mine = pl.ds(pl.multiple_of(core * half, 32), half)
     others = pl.ds(pl.multiple_of((1 - core) * half, 32), half)
     early_keep[...] = whole[mine, :tok]
     own_keep[...] = whole[mine, tok:]
-    send[...] = whole[others, :].astype(send.dtype)
+    send[...] = whole[others, :]
 
 
 def query_grads(first_block, d_raw, prior_t, keys_t, gate_rows, after, *refs):
@@ -261,11 +268,11 @@
 
 
 def add_early(keep, other, out):
-    out[...] = (keep[...] + other[:, : out.shape[1]].astype(F32)).astype(out.dtype)
+    out[...] = (keep[...].astype(F32) + other[:, : out.shape[1]].astype(F32)).astype(out.dtype)
 
 
 def add_own(keep, other, returned, after, out):
-    out[...] = (keep[...] + other[:, out.shape[1] :].astype(F32) + returned[...].astype(F32)).astype(out.dtype)
+    out[...] = (keep[...].astype(F32) + other[:, out.shape[1] :].astype(F32) + returned[...].astype(F32)).astype(out.dtype)
 
 
 def add_halves(a, b, after, out):
@@ -320,19 +327,19 @@
         out_shape=[
             kept((2 * blocks * window, TILE), BF16),
             kept((2 * blocks, TILE), F32),
-            kept((half, tok), F32),
-            kept((half, tok), F32),
+            kept((half, tok), BF16),
+            kept((half, tok), BF16),
             kept((half, 2 * tok), BF16),
         ],
         in_specs=[vmem] * 8,
         out_specs=[vmem] * 5,
         scratch_shapes=[
-            pltpu.VMEM((WIDTH, 2 * (blocks - early) * TILE), BF16),
-            pltpu.VMEM((LATENT, 2 * (blocks - early) * TILE), BF16),
+            pltpu.VMEM((WIDTH, max(1, 2 * (blocks - early)) * TILE), BF16),
+            pltpu.VMEM((LATENT, max(1, 2 * (blocks - early)) * TILE), BF16),
             pltpu.VMEM((2 * tok, PADDED), F32),
             pltpu.VMEM((2 * tok, PADDED), F32),
             pltpu.VMEM((2 * tok, LATENT), F32),
-            pltpu.VMEM((WIDTH, 2 * tok), F32),
+            pltpu.VMEM((WIDTH, 2 * tok), BF16),
         ],
         compiler_params=params,
         cost_estimate=cost(2 * columns * window * (WIDTH + LATENT), 0),

time: 29.2 us -> 28.2 us (0.966)
  Pallas kernels: 13.8 us -> 12.7 us
    pallas_call x1, Pallas kernels: 4.85 us -> 4 us  [shards(): pl.pallas_call(grads, out_shape=[kept((2 * blocks * window, TILE), BF16),...]
where the time goes in v4:
time: 28.2 us; the launch traced here: 28 us
  Pallas kernels  12.7 us (45%)
  starting transfers between devices  8 us (28%)
  waiting for transfers between devices  5.77 us (20%)
  between operations  0.76 us (3%)
  other arithmetic  0.74 us (3%)
    ppermute x2, starting transfers between devices, shifted(): lax.ppermute(value, axis, [(source, source + steps) for source in range(f...  6.3 us
    pallas_call x2, Pallas kernels, query_part(): pl.pallas_call(functools.partial(query_grads, first), out_shape=[jax.Shap...  4.68 us
    pallas_call x1, Pallas kernels, shards(): pl.pallas_call(grads, out_shape=[kept((2 * blocks * window, TILE), BF16),...  4 us
    pallas_call x1, Pallas kernels, shards(): pl.pallas_call(load, out_shape=[kept(queries.shape, BF16), kept(d_out.sha...  3.91 us
    ppermute x3, waiting for transfers between devices, exchanged(): return lax.ppermute(value, 'head', [(i, i ^ step) for i in range(group)])  3.41 us
    ppermute x2, waiting for transfers between devices, shifted(): lax.ppermute(value, axis, [(source, source + steps) for source in range(f...  2.37 us
    ppermute x3, starting transfers between devices, exchanged(): return lax.ppermute(value, 'head', [(i, i ^ step) for i in range(group)])  1.7 us
    transpose x1, other arithmetic, shards(): return (d_queries, d_gate_t.T, d_latent_t.T)  0.74 us
  transfers between devices with their start and end apart: 5, of which 4 were waited for; matrix products, arithmetic and copies ran while one was open for 0% of the time, Pallas kernels for 31%

profile of v4, /device:TPU:0, one launch (start us, length us, event | category | flops | bytes accessed | tf_op | source)
XLA Modules:
  0.0 28.0 jit_solution(16744979808259463749)
XLA Ops:
  0.6 0.0 copy-start
  0.6 0.0 copy-start.1
  0.7 5.0 %collective-permute-start = (bf16[576,128]{1,0:T(8,128)(2,1)}, bf16[576,128]{1,0:T(8,128)(2,1)S(1)}, u32[]{:S(2)}, u32[]{:S(2)}) collective-permute-start(bf16[576,128]{1,0:T(8,128)(2,1)} %bitcast.8), channel_id=1, source_target_pairs={{0,4},{4,8},{8,12},{12,16},{16,20},{20,24},{24,28},{1,5},{5,9},{9,... | collective-permute-start | bytes 442376 | tf_op jit(solution)/shard_map/ppermute | solution.py:285
  5.7 3.9 %load.1 = (bf16[128,18432]{1,0:T(8,128)(2,1)S(1)}, bf16[128,16384]{1,0:T(8,128)(2,1)S(1)}, bf16[576,3584]{1,0:T(8,128)(2,1)S(1)}, bf16[512,3584]{1,0:T(8,128)(2,1)S(1)}, bf16[576,128]{1,0:T(8,128)(2,1)S(1)}) custom-call(bf16[128,18432]{1,0:T(8,128)(2,1)} %q_hbm.1, bf16[128,16384]{1,0:T(8,128)(2,1)} %g_hbm.1, bf16[576,128]{1,0:T(8,128)(2,1)} %bitcast.9), custom_call_target="tpu_custom_call" | custom-call | bytes 8912896 | tf_op jit(solution)/shard_map/load/pallas_call | solution.py:309
  9.6 0.0 collective-permute-done.prior_t
  9.6 0.0 copy-done
  9.6 0.0 copy-done.1
  9.6 4.0 %grads.1 = (bf16[2304,256]{1,0:T(8,128)(2,1)S(1)}, f32[16,256]{1,0:T(8,128)S(1)}, bf16[288,128]{1,0:T(8,128)(2,1)S(1)}, bf16[288,128]{1,0:T(8,128)(2,1)S(1)}, bf16[288,256]{1,0:T(8,128)(2,1)S(1)}) custom-call(bf16[128,18432]{1,0:T(8,128)(2,1)S(1)} %get-tuple-element.18.q, bf16[128,16384]{1,0:T(8,128)(2,1)S(1)} %get-tuple-element.19.g, ...), custom_call_target="tpu_custom_call" | custom-call | flops 2566914048 | tf_op jit(solution)/shard_map/grads/pallas_call | solution.py:325
  13.6 0.1 collective-permute-start.1
  13.7 1.4 %collective-permute-done.1.other.after = bf16[288,256]{1,0:T(8,128)(2,1)S(1)} collective-permute-done((bf16[288,256]{1,0:T(8,128)(2,1)S(1)}, bf16[288,256]{1,0:T(8,128)(2,1)S(1)}, u32[]{:S(2)}, u32[]{:S(2)}) %collective-permute-start.1) | collective-permute-done | bytes 147488 | tf_op jit(solution)/shard_map/ppermute | solution.py:351
  15.1 1.3 %collective-permute-start.2 = (bf16[288,128]{1,0:T(8,128)(2,1)S(1)}, bf16[288,128]{1,0:T(8,128)(2,1)S(1)}, u32[]{:S(2)}, u32[]{:S(2)}) collective-permute-start(bf16[288,128]{1,0:T(8,128)(2,1)S(1)} %add_early.1), channel_id=1, source_target_pairs={{4,0},{8,4},{12,8},{16,12},{20,16},{24,20},{28,24},{5,1},{9,5},{13... | collective-permute-start | bytes 221192 | tf_op jit(solution)/shard_map/ppermute | solution.py:285
  16.4 2.6 %query_grads.2 = (bf16[128,18432]{1,0:T(8,128)(2,1)}, f32[8,128]{1,0:T(8,128)S(1)}, f32[32,128]{1,0:T(8,128)}) custom-call(bf16[2304,256]{1,0:T(8,128)(2,1)S(1)} %get-tuple-element.23.d_raw, bf16[576,128]{1,0:T(8,128)(2,1)S(1)} %collective-permute-done.prior_t, bf16[576,128]{1,0:T(8,128)(2,1)S(1)} %get-tuple-element.22.keys_t, ...), custom_call_target="tpu_custom_call" | custom-call | flops 377487360 | bytes 2359296 | tf_op jit(solution)/shard_map/query_grads/pallas_call | solution.py:365
  19.0 2.4 %collective-permute-done.2.returned = bf16[288,128]{1,0:T(8,128)(2,1)S(1)} collective-permute-done((bf16[288,128]{1,0:T(8,128)(2,1)S(1)}, bf16[288,128]{1,0:T(8,128)(2,1)S(1)}, u32[]{:S(2)}, u32[]{:S(2)}) %collective-permute-start.2) | collective-permute-done | bytes 73760 | tf_op jit(solution)/shard_map/ppermute | solution.py:285
  21.4 1.6 %collective-permute-start.3 = (bf16[288,128]{1,0:T(8,128)(2,1)S(1)}, bf16[288,128]{1,0:T(8,128)(2,1)S(1)}, u32[]{:S(2)}, u32[]{:S(2)}) collective-permute-start(bf16[288,128]{1,0:T(8,128)(2,1)S(1)} %add_own.1.after.a), channel_id=1, source_target_pairs={{0,2},{1,3},{2,0},{3,1},{4,6},{5,7},{6,4},{7,5},{8,10},{9,11},{10,... | collective-permute-start | bytes 221192 | tf_op jit(solution)/shard_map/ppermute | solution.py:351
  23.0 2.0 %query_grads.3 = (bf16[128,18432]{1,0:T(8,128)(2,1)}, f32[8,128]{1,0:T(8,128)S(1)}) custom-call(bf16[2304,256]{1,0:T(8,128)(2,1)S(1)} %get-tuple-element.23.d_raw, bf16[576,128]{1,0:T(8,128)(2,1)S(1)} %collective-permute-done.prior_t, bf16[576,128]{1,0:T(8,128)(2,1)S(1)} %get-tuple-element.22.keys_t, ...), custom_call_target="tpu_custom_call", output_to_operand_aliasing={{0}: (5, {})} | custom-call | flops 377487360 | bytes 2359296 | tf_op jit(solution)/shard_map/query_grads/pallas_call | solution.py:365
  25.0 0.8 %collective-permute-done.3.b = bf16[288,128]{1,0:T(8,128)(2,1)S(1)} collective-permute-done((bf16[288,128]{1,0:T(8,128)(2,1)S(1)}, bf16[288,128]{1,0:T(8,128)(2,1)S(1)}, u32[]{:S(2)}, u32[]{:S(2)}) %collective-permute-start.3) | collective-permute-done | bytes 73760 | tf_op jit(solution)/shard_map/ppermute | solution.py:351
  25.9 0.1 collective-permute-start.4
  26.0 1.2 %collective-permute-done.4 = bf16[288,128]{1,0:T(8,128)(2,1)S(1)} collective-permute-done((bf16[288,128]{1,0:T(8,128)(2,1)S(1)}, bf16[288,128]{1,0:T(8,128)(2,1)S(1)}, u32[]{:S(2)}, u32[]{:S(2)}) %collective-permute-start.4) | collective-permute-done | bytes 73760 | tf_op jit(solution)/shard_map/ppermute | solution.py:351
  27.2 0.7 %convert_bitcast_fusion = f32[128,576]{0,1:T(8,128)} fusion(bf16[288,128]{1,0:T(8,128)(2,1)S(1)} %collective-permute-done.4, bf16[288,128]{1,0:T(8,128)(2,1)S(1)} %add_halves.1, pred[]{:T(512)S(6)} %eq.5), kind=kLoop, calls=%fused_computation | loop fusion | flops 737280 | bytes 442369 | tf_op jit(solution)/shard_map/transpose | solution.py:393
  (3 shorter events, 0.1 us)
Async XLA Ops:
  0.6 9.0 %copy-start = (f32[128,32]{0,1:T(8,128)S(1)}, f32[128,32]{0,1:T(8,128)}, u32[]{:S(2)}) copy-start(f32[128,32]{0,1:T(8,128)} %param.7) | copy-start | bytes 49156
  0.6 9.0 %copy-start.1 = (s32[1024]{0:T(1024)S(1)}, s32[1024]{0:T(1024)}, u32[]{:S(2)}) copy-start(s32[1024]{0:T(1024)} %param.9) | copy-start | bytes 12292
  0.7 8.9 %collective-permute-start = (bf16[576,128]{1,0:T(8,128)(2,1)}, bf16[576,128]{1,0:T(8,128)(2,1)S(1)}, u32[]{:S(2)}, u32[]{:S(2)}) collective-permute-start(bf16[576,128]{1,0:T(8,128)(2,1)} %bitcast.8), channel_id=1, source_target_pairs={{0,4},{4,8},{8,12},{12,16},{16,20},{20,24},{24,28},{1,5},{5,9},{9,... | collective-permute-start | bytes 442376 | tf_op jit(solution)/shard_map/ppermute | solution.py:285
  13.6 1.4 %collective-permute-start.1 = (bf16[288,256]{1,0:T(8,128)(2,1)S(1)}, bf16[288,256]{1,0:T(8,128)(2,1)S(1)}, u32[]{:S(2)}, u32[]{:S(2)}) collective-permute-start(bf16[288,256]{1,0:T(8,128)(2,1)S(1)} %get-tuple-element.26), channel_id=1, source_target_pairs={{0,1},{1,0},{2,3},{3,2},{4,5},{5,4},{6,7},{7,6},{8,9},{9,8},{10,11... | collective-permute-start | bytes 442376 | tf_op jit(solution)/shard_map/ppermute | solution.py:351
  15.1 6.3 %collective-permute-start.2 = (bf16[288,128]{1,0:T(8,128)(2,1)S(1)}, bf16[288,128]{1,0:T(8,128)(2,1)S(1)}, u32[]{:S(2)}, u32[]{:S(2)}) collective-permute-start(bf16[288,128]{1,0:T(8,128)(2,1)S(1)} %add_early.1), channel_id=1, source_target_pairs={{4,0},{8,4},{12,8},{16,12},{20,16},{24,20},{28,24},{5,1},{9,5},{13... | collective-permute-start | bytes 221192 | tf_op jit(solution)/shard_map/ppermute | solution.py:285
  21.4 4.4 %collective-permute-start.3 = (bf16[288,128]{1,0:T(8,128)(2,1)S(1)}, bf16[288,128]{1,0:T(8,128)(2,1)S(1)}, u32[]{:S(2)}, u32[]{:S(2)}) collective-permute-start(bf16[288,128]{1,0:T(8,128)(2,1)S(1)} %add_own.1.after.a), channel_id=1, source_target_pairs={{0,2},{1,3},{2,0},{3,1},{4,6},{5,7},{6,4},{7,5},{8,10},{9,11},{10,... | collective-permute-start | bytes 221192 | tf_op jit(solution)/shard_map/ppermute | solution.py:351
  25.9 1.3 %collective-permute-start.4 = (bf16[288,128]{1,0:T(8,128)(2,1)S(1)}, bf16[288,128]{1,0:T(8,128)(2,1)S(1)}, u32[]{:S(2)}, u32[]{:S(2)}) collective-permute-start(bf16[288,128]{1,0:T(8,128)(2,1)S(1)} %add_halves.1), channel_id=1, source_target_pairs={{0,1},{1,0},{2,3},{3,2},{4,5},{5,4},{6,7},{7,6},{8,9},{9,8},{10,11... | collective-permute-start | bytes 221192 | tf_op jit(solution)/shard_map/ppermute | solution.py:351

commit v5 on v4

--- a/solution.py
+++ b/solution.py
@@ -169,7 +169,7 @@
             mean = jnp.sum(weights * d_p[:, lanes], axis=0, keepdims=True) * inverse
             gate_rows[pl.ds(n, 1), pl.ds(part * LANES, LANES)] = opened * (1.0 - opened) * mean
             gated = weights * (inverse * opened)
-            slope = gated * (d_p[:, lanes] - mean) * (SCALE - SCALE * squashed * squashed)
+            slope = weights * (inverse * opened * SCALE) * (d_p[:, lanes] - mean) * (1.0 - squashed * squashed)
             d_raw[pl.ds(n * window, window), pl.ds(part * LANES, LANES)] = slope.astype(BF16)
             gateds.append(gated.astype(BF16))
         return jnp.concatenate(gateds, axis=1)

time: 28.2 us -> 28.1 us (level)
  no operation moved by 1% of the time
where the time goes in v5:
time: 28.1 us; the launch traced here: 27.9 us
  Pallas kernels  12.6 us (45%)
  starting transfers between devices  8 us (28%)
  waiting for transfers between devices  5.77 us (21%)
  between operations  0.76 us (3%)
  other arithmetic  0.74 us (3%)
    ppermute x2, starting transfers between devices, shifted(): lax.ppermute(value, axis, [(source, source + steps) for source in range(f...  6.3 us
    pallas_call x2, Pallas kernels, query_part(): pl.pallas_call(functools.partial(query_grads, first), out_shape=[jax.Shap...  4.69 us
    pallas_call x1, Pallas kernels, shards(): pl.pallas_call(grads, out_shape=[kept((2 * blocks * window, TILE), BF16),...  3.93 us
    pallas_call x1, Pallas kernels, shards(): pl.pallas_call(load, out_shape=[kept(queries.shape, BF16), kept(d_out.sha...  3.91 us
    ppermute x3, waiting for transfers between devices, exchanged(): return lax.ppermute(value, 'head', [(i, i ^ step) for i in range(group)])  3.41 us
    ppermute x2, waiting for transfers between devices, shifted(): lax.ppermute(value, axis, [(source, source + steps) for source in range(f...  2.37 us
    ppermute x3, starting transfers between devices, exchanged(): return lax.ppermute(value, 'head', [(i, i ^ step) for i in range(group)])  1.7 us
    transpose x1, other arithmetic, shards(): return (d_queries, d_gate_t.T, d_latent_t.T)  0.74 us
  transfers between devices with their start and end apart: 5, of which 4 were waited for; matrix products, arithmetic and copies ran while one was open for 0% of the time, Pallas kernels for 31%

profile of v5, /device:TPU:0, one launch (start us, length us, event | category | flops | bytes accessed | tf_op | source)
XLA Modules:
  0.0 27.9 jit_solution(6594046358686120831)
XLA Ops:
  0.6 0.0 copy-start
  0.6 0.0 copy-start.1
  0.7 5.0 %collective-permute-start = (bf16[576,128]{1,0:T(8,128)(2,1)}, bf16[576,128]{1,0:T(8,128)(2,1)S(1)}, u32[]{:S(2)}, u32[]{:S(2)}) collective-permute-start(bf16[576,128]{1,0:T(8,128)(2,1)} %bitcast.8), channel_id=1, source_target_pairs={{0,4},{4,8},{8,12},{12,16},{16,20},{20,24},{24,28},{1,5},{5,9},{9,... | collective-permute-start | bytes 442376 | tf_op jit(solution)/shard_map/ppermute | solution.py:285
  5.7 3.9 %load.1 = (bf16[128,18432]{1,0:T(8,128)(2,1)S(1)}, bf16[128,16384]{1,0:T(8,128)(2,1)S(1)}, bf16[576,3584]{1,0:T(8,128)(2,1)S(1)}, bf16[512,3584]{1,0:T(8,128)(2,1)S(1)}, bf16[576,128]{1,0:T(8,128)(2,1)S(1)}) custom-call(bf16[128,18432]{1,0:T(8,128)(2,1)} %q_hbm.1, bf16[128,16384]{1,0:T(8,128)(2,1)} %g_hbm.1, bf16[576,128]{1,0:T(8,128)(2,1)} %bitcast.9), custom_call_target="tpu_custom_call" | custom-call | bytes 8912896 | tf_op jit(solution)/shard_map/load/pallas_call | solution.py:309
  9.6 0.0 collective-permute-done.prior_t
  9.6 0.0 copy-done
  9.6 0.0 copy-done.1
  9.6 3.9 %grads.1 = (bf16[2304,256]{1,0:T(8,128)(2,1)S(1)}, f32[16,256]{1,0:T(8,128)S(1)}, bf16[288,128]{1,0:T(8,128)(2,1)S(1)}, bf16[288,128]{1,0:T(8,128)(2,1)S(1)}, bf16[288,256]{1,0:T(8,128)(2,1)S(1)}) custom-call(bf16[128,18432]{1,0:T(8,128)(2,1)S(1)} %get-tuple-element.18.q, bf16[128,16384]{1,0:T(8,128)(2,1)S(1)} %get-tuple-element.19.g, ...), custom_call_target="tpu_custom_call" | custom-call | flops 2566914048 | tf_op jit(solution)/shard_map/grads/pallas_call | solution.py:325
  13.5 0.1 collective-permute-start.1
  13.6 1.4 %collective-permute-done.1.other.after = bf16[288,256]{1,0:T(8,128)(2,1)S(1)} collective-permute-done((bf16[288,256]{1,0:T(8,128)(2,1)S(1)}, bf16[288,256]{1,0:T(8,128)(2,1)S(1)}, u32[]{:S(2)}, u32[]{:S(2)}) %collective-permute-start.1) | collective-permute-done | bytes 147488 | tf_op jit(solution)/shard_map/ppermute | solution.py:351
  15.0 1.3 %collective-permute-start.2 = (bf16[288,128]{1,0:T(8,128)(2,1)S(1)}, bf16[288,128]{1,0:T(8,128)(2,1)S(1)}, u32[]{:S(2)}, u32[]{:S(2)}) collective-permute-start(bf16[288,128]{1,0:T(8,128)(2,1)S(1)} %add_early.1), channel_id=1, source_target_pairs={{4,0},{8,4},{12,8},{16,12},{20,16},{24,20},{28,24},{5,1},{9,5},{13... | collective-permute-start | bytes 221192 | tf_op jit(solution)/shard_map/ppermute | solution.py:285
  16.3 2.6 %query_grads.2 = (bf16[128,18432]{1,0:T(8,128)(2,1)}, f32[8,128]{1,0:T(8,128)S(1)}, f32[32,128]{1,0:T(8,128)}) custom-call(bf16[2304,256]{1,0:T(8,128)(2,1)S(1)} %get-tuple-element.23.d_raw, bf16[576,128]{1,0:T(8,128)(2,1)S(1)} %collective-permute-done.prior_t, bf16[576,128]{1,0:T(8,128)(2,1)S(1)} %get-tuple-element.22.keys_t, ...), custom_call_target="tpu_custom_call" | custom-call | flops 377487360 | bytes 2359296 | tf_op jit(solution)/shard_map/query_grads/pallas_call | solution.py:365
  19.0 2.4 %collective-permute-done.2.returned = bf16[288,128]{1,0:T(8,128)(2,1)S(1)} collective-permute-done((bf16[288,128]{1,0:T(8,128)(2,1)S(1)}, bf16[288,128]{1,0:T(8,128)(2,1)S(1)}, u32[]{:S(2)}, u32[]{:S(2)}) %collective-permute-start.2) | collective-permute-done | bytes 73760 | tf_op jit(solution)/shard_map/ppermute | solution.py:285
  21.4 1.6 %collective-permute-start.3 = (bf16[288,128]{1,0:T(8,128)(2,1)S(1)}, bf16[288,128]{1,0:T(8,128)(2,1)S(1)}, u32[]{:S(2)}, u32[]{:S(2)}) collective-permute-start(bf16[288,128]{1,0:T(8,128)(2,1)S(1)} %add_own.1.after.a), channel_id=1, source_target_pairs={{0,2},{1,3},{2,0},{3,1},{4,6},{5,7},{6,4},{7,5},{8,10},{9,11},{10,... | collective-permute-start | bytes 221192 | tf_op jit(solution)/shard_map/ppermute | solution.py:351
  22.9 2.0 %query_grads.3 = (bf16[128,18432]{1,0:T(8,128)(2,1)}, f32[8,128]{1,0:T(8,128)S(1)}) custom-call(bf16[2304,256]{1,0:T(8,128)(2,1)S(1)} %get-tuple-element.23.d_raw, bf16[576,128]{1,0:T(8,128)(2,1)S(1)} %collective-permute-done.prior_t, bf16[576,128]{1,0:T(8,128)(2,1)S(1)} %get-tuple-element.22.keys_t, ...), custom_call_target="tpu_custom_call", output_to_operand_aliasing={{0}: (5, {})} | custom-call | flops 377487360 | bytes 2359296 | tf_op jit(solution)/shard_map/query_grads/pallas_call | solution.py:365
  25.0 0.8 %collective-permute-done.3.b = bf16[288,128]{1,0:T(8,128)(2,1)S(1)} collective-permute-done((bf16[288,128]{1,0:T(8,128)(2,1)S(1)}, bf16[288,128]{1,0:T(8,128)(2,1)S(1)}, u32[]{:S(2)}, u32[]{:S(2)}) %collective-permute-start.3) | collective-permute-done | bytes 73760 | tf_op jit(solution)/shard_map/ppermute | solution.py:351
  25.8 0.1 collective-permute-start.4
  25.9 1.2 %collective-permute-done.4 = bf16[288,128]{1,0:T(8,128)(2,1)S(1)} collective-permute-done((bf16[288,128]{1,0:T(8,128)(2,1)S(1)}, bf16[288,128]{1,0:T(8,128)(2,1)S(1)}, u32[]{:S(2)}, u32[]{:S(2)}) %collective-permute-start.4) | collective-permute-done | bytes 73760 | tf_op jit(solution)/shard_map/ppermute | solution.py:351
  27.1 0.7 %convert_bitcast_fusion = f32[128,576]{0,1:T(8,128)} fusion(bf16[288,128]{1,0:T(8,128)(2,1)S(1)} %collective-permute-done.4, bf16[288,128]{1,0:T(8,128)(2,1)S(1)} %add_halves.1, pred[]{:T(512)S(6)} %eq.5), kind=kLoop, calls=%fused_computation | loop fusion | flops 737280 | bytes 442369 | tf_op jit(solution)/shard_map/transpose | solution.py:393
  (3 shorter events, 0.1 us)
Async XLA Ops:
  0.6 9.0 %copy-start = (f32[128,32]{0,1:T(8,128)S(1)}, f32[128,32]{0,1:T(8,128)}, u32[]{:S(2)}) copy-start(f32[128,32]{0,1:T(8,128)} %param.7) | copy-start | bytes 49156
  0.6 9.0 %copy-start.1 = (s32[1024]{0:T(1024)S(1)}, s32[1024]{0:T(1024)}, u32[]{:S(2)}) copy-start(s32[1024]{0:T(1024)} %param.9) | copy-start | bytes 12292
  0.7 8.9 %collective-permute-start = (bf16[576,128]{1,0:T(8,128)(2,1)}, bf16[576,128]{1,0:T(8,128)(2,1)S(1)}, u32[]{:S(2)}, u32[]{:S(2)}) collective-permute-start(bf16[576,128]{1,0:T(8,128)(2,1)} %bitcast.8), channel_id=1, source_target_pairs={{0,4},{4,8},{8,12},{12,16},{16,20},{20,24},{24,28},{1,5},{5,9},{9,... | collective-permute-start | bytes 442376 | tf_op jit(solution)/shard_map/ppermute | solution.py:285
  13.5 1.4 %collective-permute-start.1 = (bf16[288,256]{1,0:T(8,128)(2,1)S(1)}, bf16[288,256]{1,0:T(8,128)(2,1)S(1)}, u32[]{:S(2)}, u32[]{:S(2)}) collective-permute-start(bf16[288,256]{1,0:T(8,128)(2,1)S(1)} %get-tuple-element.26), channel_id=1, source_target_pairs={{0,1},{1,0},{2,3},{3,2},{4,5},{5,4},{6,7},{7,6},{8,9},{9,8},{10,11... | collective-permute-start | bytes 442376 | tf_op jit(solution)/shard_map/ppermute | solution.py:351
  15.0 6.3 %collective-permute-start.2 = (bf16[288,128]{1,0:T(8,128)(2,1)S(1)}, bf16[288,128]{1,0:T(8,128)(2,1)S(1)}, u32[]{:S(2)}, u32[]{:S(2)}) collective-permute-start(bf16[288,128]{1,0:T(8,128)(2,1)S(1)} %add_early.1), channel_id=1, source_target_pairs={{4,0},{8,4},{12,8},{16,12},{20,16},{24,20},{28,24},{5,1},{9,5},{13... | collective-permute-start | bytes 221192 | tf_op jit(solution)/shard_map/ppermute | solution.py:285
  21.4 4.4 %collective-permute-start.3 = (bf16[288,128]{1,0:T(8,128)(2,1)S(1)}, bf16[288,128]{1,0:T(8,128)(2,1)S(1)}, u32[]{:S(2)}, u32[]{:S(2)}) collective-permute-start(bf16[288,128]{1,0:T(8,128)(2,1)S(1)} %add_own.1.after.a), channel_id=1, source_target_pairs={{0,2},{1,3},{2,0},{3,1},{4,6},{5,7},{6,4},{7,5},{8,10},{9,11},{10,... | collective-permute-start | bytes 221192 | tf_op jit(solution)/shard_map/ppermute | solution.py:351
  25.8 1.3 %collective-permute-start.4 = (bf16[288,128]{1,0:T(8,128)(2,1)S(1)}, bf16[288,128]{1,0:T(8,128)(2,1)S(1)}, u32[]{:S(2)}, u32[]{:S(2)}) collective-permute-start(bf16[288,128]{1,0:T(8,128)(2,1)S(1)} %add_halves.1), channel_id=1, source_target_pairs={{0,1},{1,0},{2,3},{3,2},{4,5},{5,4},{6,7},{7,6},{8,9},{9,8},{10,11... | collective-permute-start | bytes 221192 | tf_op jit(solution)/shard_map/ppermute | solution.py:351

commit v6 on v5

--- a/solution.py
+++ b/solution.py
@@ -106,7 +106,7 @@
 def grads(
     q, g, q_turned, g_turned, prior_t, keys_t, gate_t, segments,
     d_raw, gate_rows, early_keep, own_keep, send,
-    q_turned_late, g_turned_late, acc_even, acc_odd, acc_val, whole,
+    q_turned_late, g_turned_late, acc_even, acc_odd, acc_val, side_even, side_odd, whole,
 ):
     tok, heads = gate_t.shape[1], gate_t.shape[0]
     size = 2 * TILE // heads
@@ -119,7 +119,7 @@
     key_segment = jnp.concatenate(
         [jnp.broadcast_to(row_prior, (tok, tok)).T, jnp.broadcast_to(row_own, (tok, tok)).T], axis=0
     )
-    for acc in (acc_even, acc_odd, acc_val):
+    for acc in (acc_even, acc_odd, acc_val, side_even, side_odd):
         acc[...] = jnp.zeros_like(acc)
 
     def keys_of(block):
@@ -174,16 +174,29 @@
             gateds.append(gated.astype(BF16))
         return jnp.concatenate(gateds, axis=1)
 
+    def turned_at(n):
+        if n // 2 < early:
+            return q_turned, pl.ds(n * TILE, TILE)
+        return q_turned_late, pl.ds((n - 2 * early) * TILE, TILE)
+
     def add_up(n, gated):
         block, odd = n // 2, n % 2
-        acc = acc_odd if odd else acc_even
-        acc[keys_of(block), :] += dot_nn(d_raw[pl.ds(n * window, window), :], query_tile(q, block, odd))
+        acc, side = (acc_odd, side_odd) if odd else (acc_even, side_even)
+        slope = d_raw[pl.ds(n * window, window), :]
+        tile = query_tile(q, block, odd)
+        tile = tile[:, PADDED - LATENT :] if odd else tile[:, :LATENT]
+        acc[keys_of(block), :] += dot_nn(slope, tile)
         acc_val[keys_of(block), :] += dot_nn(gated, cotangent_tile(g, block, odd))
+        above, below = block * size, 2 * tok - window - block * size
+        parts = [jnp.zeros((above, TILE), BF16)] * (above > 0) + [slope] + [jnp.zeros((below, TILE), BF16)] * (below > 0)
+        all_keys = jnp.concatenate(parts, axis=0).T
+        q_from, cols = turned_at(n)
+        side[...] += dot_nn(q_from[pl.ds(0 if odd else LATENT, ROPE), cols], all_keys)
 
     count = 2 * blocks
     raws, gateds = {}, {}
     turned = 2 * early
-    for n in range(count + 2):
+    for n in range(count + 3):
         while turned < min(count, n + 2):
             turn(q, g, turned // 2, turned % 2, q_turned_late, g_turned_late, (turned - 2 * early) * TILE)
             turned += 1
@@ -193,11 +206,11 @@
             if n % 2:
                 allowed = allowed_in((n - 1) // 2)
             gateds[n - 1] = softmax_of(n - 1, *raws.pop(n - 1), allowed)
-        if n >= 2:
-            add_up(n - 2, gateds.pop(n - 2))
-    odd_moved = pltpu.roll(acc_odd[...], PADDED - ROPE, 1)
-    summed = acc_even[...] + odd_moved + jnp.concatenate([acc_val[...], jnp.zeros((2 * tok, 2 * ROPE), F32)], axis=1)
-    whole[...] = summed.astype(BF16).T[:WIDTH]
+        if n >= 3:
+            add_up(n - 3, gateds.pop(n - 3))
+    even = jnp.concatenate([(acc_even[...] + acc_val[...]).astype(BF16).T.astype(F32), side_even[...]], axis=0)
+    odd = jnp.concatenate([side_odd[...], acc_odd[...].astype(BF16).T.astype(F32)], axis=0)
+    whole[...] = (even + odd).astype(BF16)
     core = lax.axis_index("head") % 2
     half = WIDTH // 2
     mine = pl.ds(pl.multiple_of(core * half, 32), half)
@@ -336,9 +349,11 @@
         scratch_shapes=[
             pltpu.VMEM((WIDTH, max(1, 2 * (blocks - early)) * TILE), BF16),
             pltpu.VMEM((LATENT, max(1, 2 * (blocks - early)) * TILE), BF16),
-            pltpu.VMEM((2 * tok, PADDED), F32),
-            pltpu.VMEM((2 * tok, PADDED), F32),
             pltpu.VMEM((2 * tok, LATENT), F32),
+            pltpu.VMEM((2 * tok, LATENT), F32),
+            pltpu.VMEM((2 * tok, LATENT), F32),
+            pltpu.VMEM((ROPE, 2 * tok), F32),
+            pltpu.VMEM((ROPE, 2 * tok), F32),
             pltpu.VMEM((WIDTH, 2 * tok), BF16),
         ],
         compiler_params=params,

time: 28.1 us -> 28.1 us (level)
  no operation moved by 1% of the time
where the time goes in v6:
time: 28.1 us; the launch traced here: 27.9 us
  Pallas kernels  12.6 us (45%)
  starting transfers between devices  7.99 us (28%)
  waiting for transfers between devices  5.79 us (21%)
  between operations  0.76 us (3%)
  other arithmetic  0.74 us (3%)
    ppermute x2, starting transfers between devices, shifted(): lax.ppermute(value, axis, [(source, source + steps) for source in range(f...  6.3 us
    pallas_call x2, Pallas kernels, query_part(): pl.pallas_call(functools.partial(query_grads, first), out_shape=[jax.Shap...  4.68 us
    pallas_call x1, Pallas kernels, shards(): pl.pallas_call(grads, out_shape=[kept((2 * blocks * window, TILE), BF16),...  3.94 us
    pallas_call x1, Pallas kernels, shards(): pl.pallas_call(load, out_shape=[kept(queries.shape, BF16), kept(d_out.sha...  3.91 us
    ppermute x3, waiting for transfers between devices, exchanged(): return lax.ppermute(value, 'head', [(i, i ^ step) for i in range(group)])  3.41 us
    ppermute x2, waiting for transfers between devices, shifted(): lax.ppermute(value, axis, [(source, source + steps) for source in range(f...  2.38 us
    ppermute x3, starting transfers between devices, exchanged(): return lax.ppermute(value, 'head', [(i, i ^ step) for i in range(group)])  1.69 us
    transpose x1, other arithmetic, shards(): return (d_queries, d_gate_t.T, d_latent_t.T)  0.74 us
  transfers between devices with their start and end apart: 5, of which 4 were waited for; matrix products, arithmetic and copies ran while one was open for 0% of the time, Pallas kernels for 31%

profile of v6, /device:TPU:0, one launch (start us, length us, event | category | flops | bytes accessed | tf_op | source)
XLA Modules:
  0.0 27.9 jit_solution(1484929669613332808)
XLA Ops:
  0.6 0.0 copy-start
  0.6 0.0 copy-start.1
  0.7 5.0 %collective-permute-start = (bf16[576,128]{1,0:T(8,128)(2,1)}, bf16[576,128]{1,0:T(8,128)(2,1)S(1)}, u32[]{:S(2)}, u32[]{:S(2)}) collective-permute-start(bf16[576,128]{1,0:T(8,128)(2,1)} %bitcast.8), channel_id=1, source_target_pairs={{0,4},{4,8},{8,12},{12,16},{16,20},{20,24},{24,28},{1,5},{5,9},{9,... | collective-permute-start | bytes 442376 | tf_op jit(solution)/shard_map/ppermute | solution.py:298
  5.7 3.9 %load.1 = (bf16[128,18432]{1,0:T(8,128)(2,1)S(1)}, bf16[128,16384]{1,0:T(8,128)(2,1)S(1)}, bf16[576,3584]{1,0:T(8,128)(2,1)S(1)}, bf16[512,3584]{1,0:T(8,128)(2,1)S(1)}, bf16[576,128]{1,0:T(8,128)(2,1)S(1)}) custom-call(bf16[128,18432]{1,0:T(8,128)(2,1)} %q_hbm.1, bf16[128,16384]{1,0:T(8,128)(2,1)} %g_hbm.1, bf16[576,128]{1,0:T(8,128)(2,1)} %bitcast.9), custom_call_target="tpu_custom_call" | custom-call | bytes 8912896 | tf_op jit(solution)/shard_map/load/pallas_call | solution.py:322
  9.6 0.0 collective-permute-done.prior_t
  9.6 0.0 copy-done
  9.6 0.0 copy-done.1
  9.6 3.9 %grads.1 = (bf16[2304,256]{1,0:T(8,128)(2,1)S(1)}, f32[16,256]{1,0:T(8,128)S(1)}, bf16[288,128]{1,0:T(8,128)(2,1)S(1)}, bf16[288,128]{1,0:T(8,128)(2,1)S(1)}, bf16[288,256]{1,0:T(8,128)(2,1)S(1)}) custom-call(bf16[128,18432]{1,0:T(8,128)(2,1)S(1)} %get-tuple-element.18.q, bf16[128,16384]{1,0:T(8,128)(2,1)S(1)} %get-tuple-element.19.g, ...), custom_call_target="tpu_custom_call" | custom-call | flops 2566914048 | tf_op jit(solution)/shard_map/grads/pallas_call | solution.py:338
  13.6 0.1 collective-permute-start.1
  13.6 1.4 %collective-permute-done.1.other.after = bf16[288,256]{1,0:T(8,128)(2,1)S(1)} collective-permute-done((bf16[288,256]{1,0:T(8,128)(2,1)S(1)}, bf16[288,256]{1,0:T(8,128)(2,1)S(1)}, u32[]{:S(2)}, u32[]{:S(2)}) %collective-permute-start.1) | collective-permute-done | bytes 147488 | tf_op jit(solution)/shard_map/ppermute | solution.py:366
  15.0 1.3 %collective-permute-start.2 = (bf16[288,128]{1,0:T(8,128)(2,1)S(1)}, bf16[288,128]{1,0:T(8,128)(2,1)S(1)}, u32[]{:S(2)}, u32[]{:S(2)}) collective-permute-start(bf16[288,128]{1,0:T(8,128)(2,1)S(1)} %add_early.1), channel_id=1, source_target_pairs={{4,0},{8,4},{12,8},{16,12},{20,16},{24,20},{28,24},{5,1},{9,5},{13... | collective-permute-start | bytes 221192 | tf_op jit(solution)/shard_map/ppermute | solution.py:298
  16.3 2.6 %query_grads.2 = (bf16[128,18432]{1,0:T(8,128)(2,1)}, f32[8,128]{1,0:T(8,128)S(1)}, f32[32,128]{1,0:T(8,128)}) custom-call(bf16[2304,256]{1,0:T(8,128)(2,1)S(1)} %get-tuple-element.23.d_raw, bf16[576,128]{1,0:T(8,128)(2,1)S(1)} %collective-permute-done.prior_t, bf16[576,128]{1,0:T(8,128)(2,1)S(1)} %get-tuple-element.22.keys_t, ...), custom_call_target="tpu_custom_call" | custom-call | flops 377487360 | bytes 2359296 | tf_op jit(solution)/shard_map/query_grads/pallas_call | solution.py:380
  19.0 2.4 %collective-permute-done.2.returned = bf16[288,128]{1,0:T(8,128)(2,1)S(1)} collective-permute-done((bf16[288,128]{1,0:T(8,128)(2,1)S(1)}, bf16[288,128]{1,0:T(8,128)(2,1)S(1)}, u32[]{:S(2)}, u32[]{:S(2)}) %collective-permute-start.2) | collective-permute-done | bytes 73760 | tf_op jit(solution)/shard_map/ppermute | solution.py:298
  21.4 1.5 %collective-permute-start.3 = (bf16[288,128]{1,0:T(8,128)(2,1)S(1)}, bf16[288,128]{1,0:T(8,128)(2,1)S(1)}, u32[]{:S(2)}, u32[]{:S(2)}) collective-permute-start(bf16[288,128]{1,0:T(8,128)(2,1)S(1)} %add_own.1.after.a), channel_id=1, source_target_pairs={{0,2},{1,3},{2,0},{3,1},{4,6},{5,7},{6,4},{7,5},{8,10},{9,11},{10,... | collective-permute-start | bytes 221192 | tf_op jit(solution)/shard_map/ppermute | solution.py:366
  22.9 2.0 %query_grads.3 = (bf16[128,18432]{1,0:T(8,128)(2,1)}, f32[8,128]{1,0:T(8,128)S(1)}) custom-call(bf16[2304,256]{1,0:T(8,128)(2,1)S(1)} %get-tuple-element.23.d_raw, bf16[576,128]{1,0:T(8,128)(2,1)S(1)} %collective-permute-done.prior_t, bf16[576,128]{1,0:T(8,128)(2,1)S(1)} %get-tuple-element.22.keys_t, ...), custom_call_target="tpu_custom_call", output_to_operand_aliasing={{0}: (5, {})} | custom-call | flops 377487360 | bytes 2359296 | tf_op jit(solution)/shard_map/query_grads/pallas_call | solution.py:380
  25.0 0.8 %collective-permute-done.3.b = bf16[288,128]{1,0:T(8,128)(2,1)S(1)} collective-permute-done((bf16[288,128]{1,0:T(8,128)(2,1)S(1)}, bf16[288,128]{1,0:T(8,128)(2,1)S(1)}, u32[]{:S(2)}, u32[]{:S(2)}) %collective-permute-start.3) | collective-permute-done | bytes 73760 | tf_op jit(solution)/shard_map/ppermute | solution.py:366
  25.8 0.1 collective-permute-start.4
  25.9 1.2 %collective-permute-done.4 = bf16[288,128]{1,0:T(8,128)(2,1)S(1)} collective-permute-done((bf16[288,128]{1,0:T(8,128)(2,1)S(1)}, bf16[288,128]{1,0:T(8,128)(2,1)S(1)}, u32[]{:S(2)}, u32[]{:S(2)}) %collective-permute-start.4) | collective-permute-done | bytes 73760 | tf_op jit(solution)/shard_map/ppermute | solution.py:366
  27.2 0.7 %convert_bitcast_fusion = f32[128,576]{0,1:T(8,128)} fusion(bf16[288,128]{1,0:T(8,128)(2,1)S(1)} %collective-permute-done.4, bf16[288,128]{1,0:T(8,128)(2,1)S(1)} %add_halves.1, pred[]{:T(512)S(6)} %eq.5), kind=kLoop, calls=%fused_computation | loop fusion | flops 737280 | bytes 442369 | tf_op jit(solution)/shard_map/transpose | solution.py:408
  (3 shorter events, 0.1 us)
Async XLA Ops:
  0.6 9.0 %copy-start = (f32[128,32]{0,1:T(8,128)S(1)}, f32[128,32]{0,1:T(8,128)}, u32[]{:S(2)}) copy-start(f32[128,32]{0,1:T(8,128)} %param.7) | copy-start | bytes 49156
  0.6 9.0 %copy-start.1 = (s32[1024]{0:T(1024)S(1)}, s32[1024]{0:T(1024)}, u32[]{:S(2)}) copy-start(s32[1024]{0:T(1024)} %param.9) | copy-start | bytes 12292
  0.7 8.9 %collective-permute-start = (bf16[576,128]{1,0:T(8,128)(2,1)}, bf16[576,128]{1,0:T(8,128)(2,1)S(1)}, u32[]{:S(2)}, u32[]{:S(2)}) collective-permute-start(bf16[576,128]{1,0:T(8,128)(2,1)} %bitcast.8), channel_id=1, source_target_pairs={{0,4},{4,8},{8,12},{12,16},{16,20},{20,24},{24,28},{1,5},{5,9},{9,... | collective-permute-start | bytes 442376 | tf_op jit(solution)/shard_map/ppermute | solution.py:298
  13.6 1.4 %collective-permute-start.1 = (bf16[288,256]{1,0:T(8,128)(2,1)S(1)}, bf16[288,256]{1,0:T(8,128)(2,1)S(1)}, u32[]{:S(2)}, u32[]{:S(2)}) collective-permute-start(bf16[288,256]{1,0:T(8,128)(2,1)S(1)} %get-tuple-element.26), channel_id=1, source_target_pairs={{0,1},{1,0},{2,3},{3,2},{4,5},{5,4},{6,7},{7,6},{8,9},{9,8},{10,11... | collective-permute-start | bytes 442376 | tf_op jit(solution)/shard_map/ppermute | solution.py:366
  15.0 6.3 %collective-permute-start.2 = (bf16[288,128]{1,0:T(8,128)(2,1)S(1)}, bf16[288,128]{1,0:T(8,128)(2,1)S(1)}, u32[]{:S(2)}, u32[]{:S(2)}) collective-permute-start(bf16[288,128]{1,0:T(8,128)(2,1)S(1)} %add_early.1), channel_id=1, source_target_pairs={{4,0},{8,4},{12,8},{16,12},{20,16},{24,20},{28,24},{5,1},{9,5},{13... | collective-permute-start | bytes 221192 | tf_op jit(solution)/shard_map/ppermute | solution.py:298
  21.4 4.4 %collective-permute-start.3 = (bf16[288,128]{1,0:T(8,128)(2,1)S(1)}, bf16[288,128]{1,0:T(8,128)(2,1)S(1)}, u32[]{:S(2)}, u32[]{:S(2)}) collective-permute-start(bf16[288,128]{1,0:T(8,128)(2,1)S(1)} %add_own.1.after.a), channel_id=1, source_target_pairs={{0,2},{1,3},{2,0},{3,1},{4,6},{5,7},{6,4},{7,5},{8,10},{9,11},{10,... | collective-permute-start | bytes 221192 | tf_op jit(solution)/shard_map/ppermute | solution.py:366
  25.8 1.3 %collective-permute-start.4 = (bf16[288,128]{1,0:T(8,128)(2,1)S(1)}, bf16[288,128]{1,0:T(8,128)(2,1)S(1)}, u32[]{:S(2)}, u32[]{:S(2)}) collective-permute-start(bf16[288,128]{1,0:T(8,128)(2,1)S(1)} %add_halves.1), channel_id=1, source_target_pairs={{0,1},{1,0},{2,3},{3,2},{4,5},{5,4},{6,7},{7,6},{8,9},{9,8},{10,11... | collective-permute-start | bytes 221192 | tf_op jit(solution)/shard_map/ppermute | solution.py:366

commit v7 on v6

--- a/solution.py
+++ b/solution.py
@@ -215,9 +215,10 @@
     half = WIDTH // 2
     mine = pl.ds(pl.multiple_of(core * half, 32), half)
     others = pl.ds(pl.multiple_of((1 - core) * half, 32), half)
-    early_keep[...] = whole[mine, :tok]
+    early_keep[...] = whole[others, :tok]
     own_keep[...] = whole[mine, tok:]
-    send[...] = whole[others, :]
+    send[:, :tok] = whole[mine, :tok]
+    send[:, tok:] = whole[others, tok:]
 
 
 def query_grads(first_block, d_raw, prior_t, keys_t, gate_rows, after, *refs):
@@ -292,12 +293,6 @@
     out[...] = (a[...].astype(F32) + b[...].astype(F32)).astype(out.dtype)
 
 
-def shifted(value, axis, steps):
-    count = lax.axis_size(axis)
-    first, last = (max(0, -steps), min(count, count - steps))
-    return lax.ppermute(value, axis, [(source, source + steps) for source in range(first, last)])
-
-
 def shards(queries, latent, gate, d_out, segments):
     tok = latent.shape[0]
     heads = gate.shape[1]
@@ -318,7 +313,18 @@
     def cost(multiply_adds, moved):
         return pl.CostEstimate(flops=2 * multiply_adds, bytes_accessed=moved, transcendentals=0)
 
-    prior_t = shifted(keys_t, "ctx", 1)
+    group, shards_of = lax.axis_size("head"), lax.axis_size("ctx")
+
+    def to_shard(value, steps, cross):
+        pairs = [
+            (i * group + h, (i + steps) * group + (h ^ cross))
+            for i in range(shards_of)
+            if 0 <= i + steps < shards_of
+            for h in range(group)
+        ]
+        return lax.ppermute(value, ("ctx", "head"), pairs)
+
+    prior_t = to_shard(keys_t, 1, 0)
     q, g, q_turned, g_turned, keys_t = pl.pallas_call(
         load,
         out_shape=[
@@ -360,8 +366,6 @@
         cost_estimate=cost(2 * columns * window * (WIDTH + LATENT), 0),
         name="grads",
     )(q, g, q_turned, g_turned, prior_t, keys_t, gate_t, ids)
-    group = lax.axis_size("head")
-
     def exchanged(value, step):
         return lax.ppermute(value, "head", [(i, i ^ step) for i in range(group)])
 
@@ -393,7 +397,7 @@
         )(d_raw, prior_t, keys_t, gate_rows, after, *rest)
 
     sent = exchanged(send, 1)
-    returned = shifted(small(add_early, "add_early", early_keep, sent), "ctx", -1)
+    returned = to_shard(small(add_early, "add_early", early_keep, sent), -1, 1)
     cut = (blocks + 1) // 2
     d_queries, done, d_gate_t = query_part(0, cut, sent)
     total = small(add_own, "add_own", own_keep, sent, returned, done)

time: 28.1 us -> 28 us (level)
  no operation moved by 1% of the time
where the time goes in v7:
time: 28 us; the launch traced here: 27.7 us
  Pallas kernels  12.6 us (45%)
  starting transfers between devices  8.02 us (29%)
  waiting for transfers between devices  5.59 us (20%)
  between operations  0.76 us (3%)
  other arithmetic  0.74 us (3%)
    ppermute x2, starting transfers between devices, to_shard(): return lax.ppermute(value, ('ctx', 'head'), pairs)  6.3 us
    pallas_call x2, Pallas kernels, query_part(): pl.pallas_call(functools.partial(query_grads, first), out_shape=[jax.Shap...  4.69 us
    pallas_call x1, Pallas kernels, shards(): pl.pallas_call(grads, out_shape=[kept((2 * blocks * window, TILE), BF16),...  3.95 us
    pallas_call x1, Pallas kernels, shards(): pl.pallas_call(load, out_shape=[kept(queries.shape, BF16), kept(d_out.sha...  3.91 us
    ppermute x3, waiting for transfers between devices, exchanged(): return lax.ppermute(value, 'head', [(i, i ^ step) for i in range(group)])  3.38 us
    ppermute x2, waiting for transfers between devices, to_shard(): return lax.ppermute(value, ('ctx', 'head'), pairs)  2.21 us
    ppermute x3, starting transfers between devices, exchanged(): return lax.ppermute(value, 'head', [(i, i ^ step) for i in range(group)])  1.72 us
    transpose x1, other arithmetic, shards(): return (d_queries, d_gate_t.T, d_latent_t.T)  0.74 us
  transfers between devices with their start and end apart: 5, of which 4 were waited for; matrix products, arithmetic and copies ran while one was open for 0% of the time, Pallas kernels for 31%

profile of v7, /device:TPU:0, one launch (start us, length us, event | category | flops | bytes accessed | tf_op | source)
XLA Modules:
  0.0 27.7 jit_solution(7252997871442690460)
XLA Ops:
  0.6 0.0 copy-start
  0.6 0.0 copy-start.1
  0.7 5.0 %collective-permute-start = (bf16[576,128]{1,0:T(8,128)(2,1)}, bf16[576,128]{1,0:T(8,128)(2,1)S(1)}, u32[]{:S(2)}, u32[]{:S(2)}) collective-permute-start(bf16[576,128]{1,0:T(8,128)(2,1)} %bitcast.8), channel_id=1, source_target_pairs={{0,4},{1,5},{2,6},{3,7},{4,8},{5,9},{6,10},{7,11},{8,12},{9,13},{1... | collective-permute-start | bytes 442376 | tf_op jit(solution)/shard_map/ppermute | solution.py:325
  5.7 3.9 %load.1 = (bf16[128,18432]{1,0:T(8,128)(2,1)S(1)}, bf16[128,16384]{1,0:T(8,128)(2,1)S(1)}, bf16[576,3584]{1,0:T(8,128)(2,1)S(1)}, bf16[512,3584]{1,0:T(8,128)(2,1)S(1)}, bf16[576,128]{1,0:T(8,128)(2,1)S(1)}) custom-call(bf16[128,18432]{1,0:T(8,128)(2,1)} %q_hbm.1, bf16[128,16384]{1,0:T(8,128)(2,1)} %g_hbm.1, bf16[576,128]{1,0:T(8,128)(2,1)} %bitcast.9), custom_call_target="tpu_custom_call" | custom-call | bytes 8912896 | tf_op jit(solution)/shard_map/load/pallas_call | solution.py:328
  9.6 0.0 collective-permute-done.prior_t
  9.6 0.0 copy-done
  9.6 0.0 copy-done.1
  9.6 4.0 %grads.1 = (bf16[2304,256]{1,0:T(8,128)(2,1)S(1)}, f32[16,256]{1,0:T(8,128)S(1)}, bf16[288,128]{1,0:T(8,128)(2,1)S(1)}, bf16[288,128]{1,0:T(8,128)(2,1)S(1)}, bf16[288,256]{1,0:T(8,128)(2,1)S(1)}) custom-call(bf16[128,18432]{1,0:T(8,128)(2,1)S(1)} %get-tuple-element.18.q, bf16[128,16384]{1,0:T(8,128)(2,1)S(1)} %get-tuple-element.19.g, ...), custom_call_target="tpu_custom_call" | custom-call | flops 2566914048 | tf_op jit(solution)/shard_map/grads/pallas_call | solution.py:344
  13.6 0.1 collective-permute-start.1
  13.7 1.4 %collective-permute-done.1.other.after = bf16[288,256]{1,0:T(8,128)(2,1)S(1)} collective-permute-done((bf16[288,256]{1,0:T(8,128)(2,1)S(1)}, bf16[288,256]{1,0:T(8,128)(2,1)S(1)}, u32[]{:S(2)}, u32[]{:S(2)}) %collective-permute-start.1) | collective-permute-done | bytes 147488 | tf_op jit(solution)/shard_map/ppermute | solution.py:370
  15.0 1.3 %collective-permute-start.2 = (bf16[288,128]{1,0:T(8,128)(2,1)S(1)}, bf16[288,128]{1,0:T(8,128)(2,1)S(1)}, u32[]{:S(2)}, u32[]{:S(2)}) collective-permute-start(bf16[288,128]{1,0:T(8,128)(2,1)S(1)} %add_early.1), channel_id=1, source_target_pairs={{4,1},{5,0},{6,3},{7,2},{8,5},{9,4},{10,7},{11,6},{12,9},{13,8},{1... | collective-permute-start | bytes 221192 | tf_op jit(solution)/shard_map/ppermute | solution.py:325
  16.3 2.6 %query_grads.2 = (bf16[128,18432]{1,0:T(8,128)(2,1)}, f32[8,128]{1,0:T(8,128)S(1)}, f32[32,128]{1,0:T(8,128)}) custom-call(bf16[2304,256]{1,0:T(8,128)(2,1)S(1)} %get-tuple-element.23.d_raw, bf16[576,128]{1,0:T(8,128)(2,1)S(1)} %collective-permute-done.prior_t, bf16[576,128]{1,0:T(8,128)(2,1)S(1)} %get-tuple-element.22.keys_t, ...), custom_call_target="tpu_custom_call" | custom-call | flops 377487360 | bytes 2359296 | tf_op jit(solution)/shard_map/query_grads/pallas_call | solution.py:384
  19.0 2.2 %collective-permute-done.2.returned = bf16[288,128]{1,0:T(8,128)(2,1)S(1)} collective-permute-done((bf16[288,128]{1,0:T(8,128)(2,1)S(1)}, bf16[288,128]{1,0:T(8,128)(2,1)S(1)}, u32[]{:S(2)}, u32[]{:S(2)}) %collective-permute-start.2) | collective-permute-done | bytes 73760 | tf_op jit(solution)/shard_map/ppermute | solution.py:325
  21.2 1.6 %collective-permute-start.3 = (bf16[288,128]{1,0:T(8,128)(2,1)S(1)}, bf16[288,128]{1,0:T(8,128)(2,1)S(1)}, u32[]{:S(2)}, u32[]{:S(2)}) collective-permute-start(bf16[288,128]{1,0:T(8,128)(2,1)S(1)} %add_own.1.after.a), channel_id=1, source_target_pairs={{0,2},{1,3},{2,0},{3,1},{4,6},{5,7},{6,4},{7,5},{8,10},{9,11},{10,... | collective-permute-start | bytes 221192 | tf_op jit(solution)/shard_map/ppermute | solution.py:370
  22.8 2.0 %query_grads.3 = (bf16[128,18432]{1,0:T(8,128)(2,1)}, f32[8,128]{1,0:T(8,128)S(1)}) custom-call(bf16[2304,256]{1,0:T(8,128)(2,1)S(1)} %get-tuple-element.23.d_raw, bf16[576,128]{1,0:T(8,128)(2,1)S(1)} %collective-permute-done.prior_t, bf16[576,128]{1,0:T(8,128)(2,1)S(1)} %get-tuple-element.22.keys_t, ...), custom_call_target="tpu_custom_call", output_to_operand_aliasing={{0}: (5, {})} | custom-call | flops 377487360 | bytes 2359296 | tf_op jit(solution)/shard_map/query_grads/pallas_call | solution.py:384
  24.9 0.8 %collective-permute-done.3.b = bf16[288,128]{1,0:T(8,128)(2,1)S(1)} collective-permute-done((bf16[288,128]{1,0:T(8,128)(2,1)S(1)}, bf16[288,128]{1,0:T(8,128)(2,1)S(1)}, u32[]{:S(2)}, u32[]{:S(2)}) %collective-permute-start.3) | collective-permute-done | bytes 73760 | tf_op jit(solution)/shard_map/ppermute | solution.py:370
  25.7 0.1 collective-permute-start.4
  25.8 1.2 %collective-permute-done.4 = bf16[288,128]{1,0:T(8,128)(2,1)S(1)} collective-permute-done((bf16[288,128]{1,0:T(8,128)(2,1)S(1)}, bf16[288,128]{1,0:T(8,128)(2,1)S(1)}, u32[]{:S(2)}, u32[]{:S(2)}) %collective-permute-start.4) | collective-permute-done | bytes 73760 | tf_op jit(solution)/shard_map/ppermute | solution.py:370
  27.0 0.7 %convert_bitcast_fusion = f32[128,576]{0,1:T(8,128)} fusion(bf16[288,128]{1,0:T(8,128)(2,1)S(1)} %collective-permute-done.4, bf16[288,128]{1,0:T(8,128)(2,1)S(1)} %add_halves.1, pred[]{:T(512)S(6)} %eq.5), kind=kLoop, calls=%fused_computation | loop fusion | flops 737280 | bytes 442369 | tf_op jit(solution)/shard_map/transpose | solution.py:412
  (3 shorter events, 0.1 us)
Async XLA Ops:
  0.6 9.0 %copy-start = (f32[128,32]{0,1:T(8,128)S(1)}, f32[128,32]{0,1:T(8,128)}, u32[]{:S(2)}) copy-start(f32[128,32]{0,1:T(8,128)} %param.7) | copy-start | bytes 49156
  0.6 9.0 %copy-start.1 = (s32[1024]{0:T(1024)S(1)}, s32[1024]{0:T(1024)}, u32[]{:S(2)}) copy-start(s32[1024]{0:T(1024)} %param.9) | copy-start | bytes 12292
  0.7 8.9 %collective-permute-start = (bf16[576,128]{1,0:T(8,128)(2,1)}, bf16[576,128]{1,0:T(8,128)(2,1)S(1)}, u32[]{:S(2)}, u32[]{:S(2)}) collective-permute-start(bf16[576,128]{1,0:T(8,128)(2,1)} %bitcast.8), channel_id=1, source_target_pairs={{0,4},{1,5},{2,6},{3,7},{4,8},{5,9},{6,10},{7,11},{8,12},{9,13},{1... | collective-permute-start | bytes 442376 | tf_op jit(solution)/shard_map/ppermute | solution.py:325
  13.6 1.4 %collective-permute-start.1 = (bf16[288,256]{1,0:T(8,128)(2,1)S(1)}, bf16[288,256]{1,0:T(8,128)(2,1)S(1)}, u32[]{:S(2)}, u32[]{:S(2)}) collective-permute-start(bf16[288,256]{1,0:T(8,128)(2,1)S(1)} %get-tuple-element.26), channel_id=1, source_target_pairs={{0,1},{1,0},{2,3},{3,2},{4,5},{5,4},{6,7},{7,6},{8,9},{9,8},{10,11... | collective-permute-start | bytes 442376 | tf_op jit(solution)/shard_map/ppermute | solution.py:370
  15.0 6.1 %collective-permute-start.2 = (bf16[288,128]{1,0:T(8,128)(2,1)S(1)}, bf16[288,128]{1,0:T(8,128)(2,1)S(1)}, u32[]{:S(2)}, u32[]{:S(2)}) collective-permute-start(bf16[288,128]{1,0:T(8,128)(2,1)S(1)} %add_early.1), channel_id=1, source_target_pairs={{4,1},{5,0},{6,3},{7,2},{8,5},{9,4},{10,7},{11,6},{12,9},{13,8},{1... | collective-permute-start | bytes 221192 | tf_op jit(solution)/shard_map/ppermute | solution.py:325
  21.2 4.4 %collective-permute-start.3 = (bf16[288,128]{1,0:T(8,128)(2,1)S(1)}, bf16[288,128]{1,0:T(8,128)(2,1)S(1)}, u32[]{:S(2)}, u32[]{:S(2)}) collective-permute-start(bf16[288,128]{1,0:T(8,128)(2,1)S(1)} %add_own.1.after.a), channel_id=1, source_target_pairs={{0,2},{1,3},{2,0},{3,1},{4,6},{5,7},{6,4},{7,5},{8,10},{9,11},{10,... | collective-permute-start | bytes 221192 | tf_op jit(solution)/shard_map/ppermute | solution.py:370
  25.7 1.3 %collective-permute-start.4 = (bf16[288,128]{1,0:T(8,128)(2,1)S(1)}, bf16[288,128]{1,0:T(8,128)(2,1)S(1)}, u32[]{:S(2)}, u32[]{:S(2)}) collective-permute-start(bf16[288,128]{1,0:T(8,128)(2,1)S(1)} %add_halves.1), channel_id=1, source_target_pairs={{0,1},{1,0},{2,3},{3,2},{4,5},{5,4},{6,7},{7,6},{8,9},{9,8},{10,11... | collective-permute-start | bytes 221192 | tf_op jit(solution)/shard_map/ppermute | solution.py:370

commit v8 on v7

--- a/solution.py
+++ b/solution.py
@@ -289,6 +289,11 @@
     out[...] = (keep[...].astype(F32) + other[:, out.shape[1] :].astype(F32) + returned[...].astype(F32)).astype(out.dtype)
 
 
+def join(a, b, after, out):
+    out[pl.ds(0, a.shape[0]), :] = a[...]
+    out[pl.ds(a.shape[0], a.shape[0]), :] = b[...]
+
+
 def add_halves(a, b, after, out):
     out[...] = (a[...].astype(F32) + b[...].astype(F32)).astype(out.dtype)
 
@@ -403,12 +408,24 @@
     total = small(add_own, "add_own", own_keep, sent, returned, done)
     d_queries, done = query_part(cut, blocks - cut, total, d_queries)
     step = 2
-    while step < group:
+    while 2 * step < group:
         total = small(add_halves, "add_halves", total, exchanged(total, step), done)
         step *= 2
-    other = exchanged(total, 1)
+    both = pl.pallas_call(
+        join,
+        out_shape=kept((2 * half, tok), BF16),
+        in_specs=[vmem, vmem, hbm],
+        out_specs=vmem,
+        compiler_params=params,
+        name="join",
+    )(total, exchanged(total, step ^ 1), done)
+    given = exchanged(both, 1)
+    own_half = both[:half].astype(F32) + given[half:].astype(F32)
+    other_half = both[half:].astype(F32) + given[:half].astype(F32)
     first = lax.axis_index("head") % 2 == 0
-    d_latent_t = jnp.where(first, jnp.concatenate([total, other]), jnp.concatenate([other, total])).astype(F32)
+    d_latent_t = jnp.where(
+        first, jnp.concatenate([own_half, other_half]), jnp.concatenate([other_half, own_half])
+    )
     return d_queries, d_gate_t.T, d_latent_t.T
 
 

time: 28 us -> 28 us (level)
  no operation moved by 1% of the time
where the time goes in v8:
time: 28 us; the launch traced here: 27.8 us
  Pallas kernels  12.6 us (45%)
  starting transfers between devices  7.87 us (28%)
  waiting for transfers between devices  5.77 us (21%)
  other arithmetic  0.77 us (3%)
  between operations  0.74 us (3%)
    ppermute x2, starting transfers between devices, to_shard(): return lax.ppermute(value, ('ctx', 'head'), pairs)  6.3 us
    pallas_call x2, Pallas kernels, query_part(): pl.pallas_call(functools.partial(query_grads, first), out_shape=[jax.Shap...  4.68 us
    pallas_call x1, Pallas kernels, shards(): pl.pallas_call(grads, out_shape=[kept((2 * blocks * window, TILE), BF16),...  3.95 us
    pallas_call x1, Pallas kernels, shards(): pl.pallas_call(load, out_shape=[kept(queries.shape, BF16), kept(d_out.sha...  3.91 us
    ppermute x3, waiting for transfers between devices, exchanged(): return lax.ppermute(value, 'head', [(i, i ^ step) for i in range(group)])  3.56 us
    ppermute x2, waiting for transfers between devices, to_shard(): return lax.ppermute(value, ('ctx', 'head'), pairs)  2.21 us
    ppermute x3, starting transfers between devices, exchanged(): return lax.ppermute(value, 'head', [(i, i ^ step) for i in range(group)])  1.57 us
    transpose x1, other arithmetic, shards(): return (d_queries, d_gate_t.T, d_latent_t.T)  0.74 us
  transfers between devices with their start and end apart: 5, of which 4 were waited for; matrix products, arithmetic and copies ran while one was open for 0% of the time, Pallas kernels for 31%

profile of v8, /device:TPU:0, one launch (start us, length us, event | category | flops | bytes accessed | tf_op | source)
XLA Modules:
  0.0 27.8 jit_solution(9443696024661634288)
XLA Ops:
  0.6 0.0 copy-start
  0.6 0.0 copy-start.1
  0.7 5.0 %collective-permute-start = (bf16[576,128]{1,0:T(8,128)(2,1)}, bf16[576,128]{1,0:T(8,128)(2,1)S(1)}, u32[]{:S(2)}, u32[]{:S(2)}) collective-permute-start(bf16[576,128]{1,0:T(8,128)(2,1)} %bitcast.8), channel_id=1, source_target_pairs={{0,4},{1,5},{2,6},{3,7},{4,8},{5,9},{6,10},{7,11},{8,12},{9,13},{1... | collective-permute-start | bytes 442376 | tf_op jit(solution)/shard_map/ppermute | solution.py:330
  5.7 3.9 %load.1 = (bf16[128,18432]{1,0:T(8,128)(2,1)S(1)}, bf16[128,16384]{1,0:T(8,128)(2,1)S(1)}, bf16[576,3584]{1,0:T(8,128)(2,1)S(1)}, bf16[512,3584]{1,0:T(8,128)(2,1)S(1)}, bf16[576,128]{1,0:T(8,128)(2,1)S(1)}) custom-call(bf16[128,18432]{1,0:T(8,128)(2,1)} %q_hbm.1, bf16[128,16384]{1,0:T(8,128)(2,1)} %g_hbm.1, bf16[576,128]{1,0:T(8,128)(2,1)} %bitcast.9), custom_call_target="tpu_custom_call" | custom-call | bytes 8912896 | tf_op jit(solution)/shard_map/load/pallas_call | solution.py:333
  9.6 0.0 collective-permute-done.prior_t
  9.6 0.0 copy-done
  9.6 0.0 copy-done.1
  9.6 4.0 %grads.1 = (bf16[2304,256]{1,0:T(8,128)(2,1)S(1)}, f32[16,256]{1,0:T(8,128)S(1)}, bf16[288,128]{1,0:T(8,128)(2,1)S(1)}, bf16[288,128]{1,0:T(8,128)(2,1)S(1)}, bf16[288,256]{1,0:T(8,128)(2,1)S(1)}) custom-call(bf16[128,18432]{1,0:T(8,128)(2,1)S(1)} %get-tuple-element.18.q, bf16[128,16384]{1,0:T(8,128)(2,1)S(1)} %get-tuple-element.19.g, ...), custom_call_target="tpu_custom_call" | custom-call | flops 2566914048 | tf_op jit(solution)/shard_map/grads/pallas_call | solution.py:349
  13.6 0.1 collective-permute-start.1
  13.7 1.4 %collective-permute-done.1.other.after = bf16[288,256]{1,0:T(8,128)(2,1)S(1)} collective-permute-done((bf16[288,256]{1,0:T(8,128)(2,1)S(1)}, bf16[288,256]{1,0:T(8,128)(2,1)S(1)}, u32[]{:S(2)}, u32[]{:S(2)}) %collective-permute-start.1) | collective-permute-done | bytes 147488 | tf_op jit(solution)/shard_map/ppermute | solution.py:375
  15.0 1.3 %collective-permute-start.2 = (bf16[288,128]{1,0:T(8,128)(2,1)S(1)}, bf16[288,128]{1,0:T(8,128)(2,1)S(1)}, u32[]{:S(2)}, u32[]{:S(2)}) collective-permute-start(bf16[288,128]{1,0:T(8,128)(2,1)S(1)} %add_early.1), channel_id=1, source_target_pairs={{4,1},{5,0},{6,3},{7,2},{8,5},{9,4},{10,7},{11,6},{12,9},{13,8},{1... | collective-permute-start | bytes 221192 | tf_op jit(solution)/shard_map/ppermute | solution.py:330
  16.3 2.6 %query_grads.2 = (bf16[128,18432]{1,0:T(8,128)(2,1)}, f32[8,128]{1,0:T(8,128)S(1)}, f32[32,128]{1,0:T(8,128)}) custom-call(bf16[2304,256]{1,0:T(8,128)(2,1)S(1)} %get-tuple-element.23.d_raw, bf16[576,128]{1,0:T(8,128)(2,1)S(1)} %collective-permute-done.prior_t, bf16[576,128]{1,0:T(8,128)(2,1)S(1)} %get-tuple-element.22.keys_t, ...), custom_call_target="tpu_custom_call" | custom-call | flops 377487360 | bytes 2359296 | tf_op jit(solution)/shard_map/query_grads/pallas_call | solution.py:389
  19.0 2.2 %collective-permute-done.2.returned = bf16[288,128]{1,0:T(8,128)(2,1)S(1)} collective-permute-done((bf16[288,128]{1,0:T(8,128)(2,1)S(1)}, bf16[288,128]{1,0:T(8,128)(2,1)S(1)}, u32[]{:S(2)}, u32[]{:S(2)}) %collective-permute-start.2) | collective-permute-done | bytes 73760 | tf_op jit(solution)/shard_map/ppermute | solution.py:330
  21.2 1.3 %collective-permute-start.3 = (bf16[288,128]{1,0:T(8,128)(2,1)S(1)}, bf16[288,128]{1,0:T(8,128)(2,1)S(1)}, u32[]{:S(2)}, u32[]{:S(2)}) collective-permute-start(bf16[288,128]{1,0:T(8,128)(2,1)S(1)} %add_own.1.after.a), channel_id=1, source_target_pairs={{0,3},{1,2},{2,1},{3,0},{4,7},{5,6},{6,5},{7,4},{8,11},{9,10},{10,... | collective-permute-start | bytes 221192 | tf_op jit(solution)/shard_map/ppermute | solution.py:375
  22.5 2.0 %query_grads.3 = (bf16[128,18432]{1,0:T(8,128)(2,1)}, f32[8,128]{1,0:T(8,128)S(1)}) custom-call(bf16[2304,256]{1,0:T(8,128)(2,1)S(1)} %get-tuple-element.23.d_raw, bf16[576,128]{1,0:T(8,128)(2,1)S(1)} %collective-permute-done.prior_t, bf16[576,128]{1,0:T(8,128)(2,1)S(1)} %get-tuple-element.22.keys_t, ...), custom_call_target="tpu_custom_call", output_to_operand_aliasing={{0}: (5, {})} | custom-call | flops 377487360 | bytes 2359296 | tf_op jit(solution)/shard_map/query_grads/pallas_call | solution.py:389
  24.6 1.0 %collective-permute-done.3.b = bf16[288,128]{1,0:T(8,128)(2,1)S(1)} collective-permute-done((bf16[288,128]{1,0:T(8,128)(2,1)S(1)}, bf16[288,128]{1,0:T(8,128)(2,1)S(1)}, u32[]{:S(2)}, u32[]{:S(2)}) %collective-permute-start.3) | collective-permute-done | bytes 73760 | tf_op jit(solution)/shard_map/ppermute | solution.py:375
  25.6 0.2 collective-permute-start.4
  25.8 1.2 %collective-permute-done.4 = bf16[576,128]{1,0:T(8,128)(2,1)S(1)} collective-permute-done((bf16[576,128]{1,0:T(8,128)(2,1)S(1)}, bf16[576,128]{1,0:T(8,128)(2,1)S(1)}, u32[]{:S(2)}, u32[]{:S(2)}) %collective-permute-start.4) | collective-permute-done | bytes 147488 | tf_op jit(solution)/shard_map/ppermute | solution.py:375
  27.0 0.7 %fusion = f32[128,576]{0,1:T(8,128)} fusion(f32[288,128]{1,0:T(8,128)S(1)} %get-tuple-element.34, f32[288,128]{1,0:T(8,128)S(1)} %get-tuple-element.33, pred[]{:T(512)S(6)} %eq.5), kind=kLoop, calls=%fused_computation.1 | loop fusion | flops 221184 | bytes 589825 | tf_op jit(solution)/shard_map/transpose | solution.py:429
  (4 shorter events, 0.1 us)
Async XLA Ops:
  0.6 9.0 %copy-start = (f32[128,32]{0,1:T(8,128)S(1)}, f32[128,32]{0,1:T(8,128)}, u32[]{:S(2)}) copy-start(f32[128,32]{0,1:T(8,128)} %param.7) | copy-start | bytes 49156
  0.6 9.0 %copy-start.1 = (s32[1024]{0:T(1024)S(1)}, s32[1024]{0:T(1024)}, u32[]{:S(2)}) copy-start(s32[1024]{0:T(1024)} %param.9) | copy-start | bytes 12292
  0.7 8.9 %collective-permute-start = (bf16[576,128]{1,0:T(8,128)(2,1)}, bf16[576,128]{1,0:T(8,128)(2,1)S(1)}, u32[]{:S(2)}, u32[]{:S(2)}) collective-permute-start(bf16[576,128]{1,0:T(8,128)(2,1)} %bitcast.8), channel_id=1, source_target_pairs={{0,4},{1,5},{2,6},{3,7},{4,8},{5,9},{6,10},{7,11},{8,12},{9,13},{1... | collective-permute-start | bytes 442376 | tf_op jit(solution)/shard_map/ppermute | solution.py:330
  13.6 1.4 %collective-permute-start.1 = (bf16[288,256]{1,0:T(8,128)(2,1)S(1)}, bf16[288,256]{1,0:T(8,128)(2,1)S(1)}, u32[]{:S(2)}, u32[]{:S(2)}) collective-permute-start(bf16[288,256]{1,0:T(8,128)(2,1)S(1)} %get-tuple-element.26), channel_id=1, source_target_pairs={{0,1},{1,0},{2,3},{3,2},{4,5},{5,4},{6,7},{7,6},{8,9},{9,8},{10,11... | collective-permute-start | bytes 442376 | tf_op jit(solution)/shard_map/ppermute | solution.py:375
  15.0 6.1 %collective-permute-start.2 = (bf16[288,128]{1,0:T(8,128)(2,1)S(1)}, bf16[288,128]{1,0:T(8,128)(2,1)S(1)}, u32[]{:S(2)}, u32[]{:S(2)}) collective-permute-start(bf16[288,128]{1,0:T(8,128)(2,1)S(1)} %add_early.1), channel_id=1, source_target_pairs={{4,1},{5,0},{6,3},{7,2},{8,5},{9,4},{10,7},{11,6},{12,9},{13,8},{1... | collective-permute-start | bytes 221192 | tf_op jit(solution)/shard_map/ppermute | solution.py:330
  21.2 4.3 %collective-permute-start.3 = (bf16[288,128]{1,0:T(8,128)(2,1)S(1)}, bf16[288,128]{1,0:T(8,128)(2,1)S(1)}, u32[]{:S(2)}, u32[]{:S(2)}) collective-permute-start(bf16[288,128]{1,0:T(8,128)(2,1)S(1)} %add_own.1.after.a), channel_id=1, source_target_pairs={{0,3},{1,2},{2,1},{3,0},{4,7},{5,6},{6,5},{7,4},{8,11},{9,10},{10,... | collective-permute-start | bytes 221192 | tf_op jit(solution)/shard_map/ppermute | solution.py:375
  25.6 1.4 %collective-permute-start.4 = (bf16[576,128]{1,0:T(8,128)(2,1)S(1)}, bf16[576,128]{1,0:T(8,128)(2,1)S(1)}, u32[]{:S(2)}, u32[]{:S(2)}) collective-permute-start(bf16[576,128]{1,0:T(8,128)(2,1)S(1)} %join.1), channel_id=1, source_target_pairs={{0,1},{1,0},{2,3},{3,2},{4,5},{5,4},{6,7},{7,6},{8,9},{9,8},{10,11... | collective-permute-start | bytes 442376 | tf_op jit(solution)/shard_map/ppermute | solution.py:375
